TPU v7x, 32 devices: a whole 2x2x4 slice. The times are simulated.
32 devices in a mesh: ctx: 8 (over z, y), kvh: 4 (over x, core).
Axes of the slice: x: 2, y: 2, z: 4, core: 2. Of those that a mesh axis runs over, the one named last changes fastest.
Arguments:
- queries: bfloat16 [64, 64, 4, 1024], P('ctx', None, 'kvh'), may hold values from -92 to 92
- resp_keys: bfloat16 [64, 64, 4, 128], P('ctx', None, 'kvh'), may hold values from -6 to 6
- resp_values: bfloat16 [64, 64, 4, 128], P('ctx', None, 'kvh'), may hold values from -6 to 6
- prefix_keys: bfloat16 [32768, 4, 128], P('ctx', 'kvh'), may hold values from -6 to 6
- prefix_values: bfloat16 [32768, 4, 128], P('ctx', 'kvh'), may hold values from -6 to 6
- prefix_len: int32 [4], replicated, may hold values from 2048 to 8192, as said below
- prompt_of: int32 [64], replicated, may hold values from 0 to 3, as said below
- out_weight: bfloat16 [4096, 8192], P('kvh', 'ctx'), may hold values from -0.09375 to 0.09375
Outputs:
- attended: bfloat16 [64, 64, 4, 1024], P('ctx', None, 'kvh')
- projected: bfloat16 [4096, 8192], P('ctx', 'kvh')
Inputs may be any that keep to these rules, and one draw needn't show every extreme that they name: `prefix_len`: every prompt's length lies in the range and one prompt has exactly 8192. `prompt_of`: every prompt is named by 16 responses; the 8 responses of one index of ctx name each prompt at most 2 times, and some prompt exactly 2 times on every index.
All inputs are finite; a program needn't handle non-finite values.
Results may differ from a plain program's by a relative error of at most 0.038.
Values may be sent and summed in bfloat16 or wider, within the bound.
No kernel may reach another device: no remote copies, remote signals or barrier semaphores. Data moves between devices by JAX's collectives and lax.ppermute only.
A program may use at most 192 MiB of HBM per device.

v0:
```python
import math

import jax
import jax.numpy as jnp
from jax import lax
from jax.sharding import PartitionSpec as P

MASKED = -1e30


def partial_block(query_rows, shard_keys, shard_values, live):
    scores = jnp.einsum(
        "bhd,sd->bhs", query_rows, shard_keys, preferred_element_type=jnp.float32
    ) * (1.0 / math.sqrt(shard_keys.shape[-1]))
    scores = jnp.where(live, scores, MASKED)
    peak_score = jnp.max(scores, axis=-1)
    weights = jnp.where(live, jnp.exp(scores - peak_score[..., None]), 0.0)
    totals = jnp.sum(weights, axis=-1)
    mixed_out = jnp.einsum(
        "bhs,sd->bhd",
        weights.astype(jnp.bfloat16),
        shard_values,
        preferred_element_type=jnp.float32,
    )
    return (mixed_out, peak_score, totals)


def holder_attend(incoming, shard_keys, shard_values, live_slots):
    sources, slot_rows, tokens_each, feature_width = incoming.shape
    head_size = shard_keys.shape[-1]
    head_count = feature_width // head_size
    total_rows = sources * slot_rows * tokens_each
    block_rows = math.gcd(512, total_rows)
    block_count = total_rows // block_rows
    stacked = incoming.reshape(block_count, block_rows, head_count, head_size)

    def one_block(query_rows):
        mixed_out, peak_score, totals = partial_block(
            query_rows, shard_keys, shard_values, live_slots[None, None, :]
        )
        return (
            mixed_out.astype(jnp.bfloat16).reshape(block_rows, feature_width),
            peak_score,
            totals,
        )

    mixed_out, peak_score, totals = lax.map(one_block, stacked)
    return (
        mixed_out.reshape(sources, slot_rows, tokens_each, feature_width),
        peak_score.reshape(sources, slot_rows, tokens_each, head_count),
        totals.reshape(sources, slot_rows, tokens_each, head_count),
    )


def return_partials(parts):
    return (
        lax.all_to_all(parts[0], "ctx", split_axis=0, concat_axis=0, tiled=True),
        lax.all_to_all(
            parts[1].astype(jnp.bfloat16), "ctx", split_axis=0, concat_axis=0, tiled=True
        ).astype(jnp.float32),
        lax.all_to_all(
            parts[2].astype(jnp.bfloat16), "ctx", split_axis=0, concat_axis=0, tiled=True
        ).astype(jnp.float32),
    )


def local(
    queries, resp_keys, resp_values, prefix_keys, prefix_values, prefix_len, prompt_of, out_weight
):
    ctx_count = lax.axis_size("ctx")
    position = lax.axis_index("ctx")
    own_queries = queries[:, :, 0]
    own_keys = resp_keys[:, :, 0]
    own_values = resp_values[:, :, 0]
    shard_keys = prefix_keys[:, 0]
    shard_values = prefix_values[:, 0]
    resp_count, tokens_each, feature_width = own_queries.shape
    slot_count, head_size = shard_keys.shape
    head_count = feature_width // head_size
    prompt_count = prefix_len.shape[0]
    holders = ctx_count // prompt_count
    capacity = max(1, resp_count // prompt_count)
    own_prompts = lax.dynamic_slice_in_dim(prompt_of, position * resp_count, resp_count, 0)
    local_ids = jnp.arange(resp_count, dtype=jnp.int32)
    same_prompt = own_prompts[None, :] == own_prompts[:, None]
    rank_within = jnp.sum(same_prompt & (local_ids[None, :] < local_ids[:, None]), axis=1)
    dest_prompt = jnp.arange(ctx_count, dtype=jnp.int32) // holders
    matches = (own_prompts[None, None, :] == dest_prompt[:, None, None]) & (
        rank_within[None, None, :] == jnp.arange(capacity, dtype=jnp.int32)[None, :, None]
    )
    chosen = jnp.sum(jnp.where(matches, local_ids[None, None, :], 0), axis=-1)
    present = jnp.any(matches, axis=-1)
    outgoing = jnp.where(
        present[:, :, None, None], own_queries[chosen], jnp.zeros((), jnp.bfloat16)
    )
    my_prompt = position // holders
    offset = position % holders * slot_count
    live_slots = offset + jnp.arange(slot_count, dtype=jnp.int32) < prefix_len[my_prompt]
    arrived = lax.all_to_all(outgoing, "ctx", split_axis=0, concat_axis=0, tiled=True)
    back_mixed, back_peak, back_totals = return_partials(
        holder_attend(arrived, shard_keys, shard_values, live_slots)
    )
    pick_rows = (
        own_prompts[:, None] * holders + jnp.arange(holders, dtype=jnp.int32)[None, :]
    ) * capacity + rank_within[:, None]
    got_mixed = back_mixed.reshape(ctx_count * capacity, tokens_each, feature_width)[pick_rows]
    got_peak = back_peak.reshape(ctx_count * capacity, tokens_each, head_count)[pick_rows]
    got_totals = back_totals.reshape(ctx_count * capacity, tokens_each, head_count)[pick_rows]
    own_rows = own_queries.reshape(resp_count, tokens_each, head_count, head_size)
    causal = jnp.arange(tokens_each)[:, None] >= jnp.arange(tokens_each)[None, :]
    own_mixed, own_peak, own_totals = jax.vmap(partial_block, in_axes=(0, 0, 0, None))(
        own_rows, own_keys, own_values, causal[:, None, :]
    )
    highest = jnp.maximum(own_peak, jnp.max(got_peak, axis=1))
    own_scale = jnp.exp(own_peak - highest)
    far_scale = jnp.exp(got_peak - highest[:, None])
    far_mixed = got_mixed.reshape(resp_count, holders, tokens_each, head_count, head_size).astype(
        jnp.float32
    )
    numerator = own_scale[..., None] * own_mixed + jnp.sum(far_scale[..., None] * far_mixed, axis=1)
    denominator = own_scale * own_totals + jnp.sum(far_scale * got_totals, axis=1)
    attended = (
        (numerator / denominator[..., None])
        .astype(jnp.bfloat16)
        .reshape(resp_count, tokens_each, feature_width)
    )
    flat_rows = attended.reshape(resp_count * tokens_each, feature_width)
    partial_terms = jnp.dot(
        flat_rows,
        lax.all_gather(out_weight, "ctx", axis=1, tiled=True),
        preferred_element_type=jnp.float32,
    )
    projected = lax.psum_scatter(
        partial_terms.astype(jnp.bfloat16), "kvh", scatter_dimension=1, tiled=True
    )
    return (attended[:, :, None, :], projected)


def solution(mesh):
    in_specs = (
        P("ctx", None, "kvh", None),
        P("ctx", None, "kvh", None),
        P("ctx", None, "kvh", None),
        P("ctx", "kvh", None),
        P("ctx", "kvh", None),
        P(),
        P(),
        P("kvh", "ctx"),
    )
    out_specs = (P("ctx", None, "kvh", None), P("ctx", "kvh"))
    return jax.shard_map(local, mesh=mesh, in_specs=in_specs, out_specs=out_specs, check_vma=False)
```

profile of v0, /device:TPU:0, one launch (start us, length us, event | category | flops | bytes accessed | tf_op | source)
XLA Modules:
  0.0 441.2 jit_solution(17128819708730034026)
XLA Ops:
  7.2 1.3 broadcast_multiply_fusion
  8.5 0.2 convert_reduce_fusion
  8.7 0.1 fusion.33
  8.9 0.2 and_reduce_fusion
  9.0 0.2 copy-done.9
  9.2 0.1 copy.86
  9.3 0.1 reshape.239
  9.4 0.1 copy.85
  9.5 1.9 gather_fusion
  11.4 1.6 broadcast_select_fusion
  13.0 7.3 %all-to-all-start = ((bf16[8,2,64,1024]{3,2,1,0:T(8,128)(2,1)}), bf16[8,2,64,1024]{3,2,1,0:T(8,128)(2,1)S(1)}, u32[]{:S(2)}, u32[]{:S(2)}) async-start(bf16[8,2,64,1024]{3,2,1,0:T(8,128)(2,1)} %broadcast_select_fusion), calls=%async_computation | async-start | bytes 4194304 | tf_op jit(solution)/shard_map/all_to_all | solution.py:99
  20.3 0.7 all-gather.2.cloned.1.call-update
  21.1 0.4 copy-done.5
  21.5 1.3 copy.87
  22.8 0.7 dynamic_slice.10
  23.4 84.2 %all-to-all-done = bf16[8,2,64,1024]{3,2,1,0:T(8,128)(2,1)S(1)} async-done(((bf16[8,2,64,1024]{3,2,1,0:T(8,128)(2,1)}), bf16[8,2,64,1024]{3,2,1,0:T(8,128)(2,1)S(1)}, u32[]{:S(2)}, u32[]{:S(2)}) %all-to-all-start) | async-done | bytes 2097184 | tf_op jit(solution)/shard_map/all_to_all | solution.py:99
  107.6 1.9 copy.110
  109.6 151.0 %while.15 = (s32[]{:T(128)}, bf16[2,512,1024]{2,1,0:T(8,128)(2,1)}, bf16[2,512,8]{1,2,0:T(8,128)(2,1)S(1)}, bf16[2,512,8]{1,2,0:T(8,128)(2,1)S(1)}, bf16[2,512,8...) while((s32[]{:T(128)}, bf16[2,512,1024]{2,1,0:T(8,128)(2,1)}, ...), condition=%wide.region_7.8_spmd.clone, body=%wide.region_4.7_spmd.clone.sunk | while | flops 8808562688 | bytes 211935872 | solution.py:47
  109.6 1.3 constant_dynamic-slice_fusion.2
  110.9 0.7 add_compare_fusion.2
  111.5 23.9 %fusion.47 = (f32[512,8]{0,1:T(8,128)S(1)}, f32[512,8,4096]{2,0,1:T(8,128)}) fusion(pred[4096]{0:T(1024)(128)(4,1)S(1)} %add_compare_fusion.2, bf16[4096,128]{1,0:T(8,128)(2,1)S(1)} %get-tuple-element.252, bf16[1,512,8,128]{3,2,1,0:T(8,128)(2,1)S(1)} %constant_dynamic-slice_fusion.2), kind=kOutput, calls=%fused_computation.7.clone.1 | convolution fusion | flops 4345294848 | bytes 69226496 | tf_op jit(solution)/shard_map/while/body/eval_jaxpr/bhd,sd->bhs/dot_general | solution.py:12
  135.4 24.0 %fusion.49 = bf16[512,8]{0,1:T(8,128)(2,1)S(1)} fusion(f32[512,8,4096]{2,0,1:T(8,128)} %get-tuple-element.225, f32[512,8]{0,1:T(8,128)S(1)} %get-tuple-element.226, pred[4096]{0:T(1024)(128)(4,1)S(1)} %add_compare_fusion.2), kind=kLoop, calls=%fused_computation.8.clone.1 | loop fusion | flops 83881984 | bytes 67137536 | tf_op jit(solution)/shard_map/while/body/eval_jaxpr/reduce_sum | solution.py:18
  159.5 24.9 %fusion.48 = bf16[512,8,128]{0,2,1:T(8,128)(2,1)S(1)} fusion(f32[512,8,4096]{2,0,1:T(8,128)} %get-tuple-element.225, f32[512,8]{0,1:T(8,128)S(1)} %get-tuple-element.226, pred[4096]{0:T(1024)(128)(4,1)S(1)} %add_compare_fusion.2, bf16[4096,128]{0,1:T(8,128)(2,1)} %get-tuple-element.253), kind=kOutput, calls=%fused_computation.12.clone.1 | convolution fusion | flops 4379377664 | bytes 69226496 | tf_op jit(solution)/shard_map/while/body/eval_jaxpr/bhs,sd->bhd/dot_general | solution.py:19
  184.4 0.5 copy.128
  184.9 1.0 constant_dynamic-update-slice_fusion.2
  186.0 1.3 constant_dynamic-slice_fusion.2
  187.3 0.7 add_compare_fusion.2
  187.9 23.9 %fusion.47 = (f32[512,8]{0,1:T(8,128)S(1)}, f32[512,8,4096]{2,0,1:T(8,128)}) fusion(pred[4096]{0:T(1024)(128)(4,1)S(1)} %add_compare_fusion.2, bf16[4096,128]{1,0:T(8,128)(2,1)S(1)} %get-tuple-element.252, bf16[1,512,8,128]{3,2,1,0:T(8,128)(2,1)S(1)} %constant_dynamic-slice_fusion.2), kind=kOutput, calls=%fused_computation.7.clone.1 | convolution fusion | flops 4345294848 | bytes 69226496 | tf_op jit(solution)/shard_map/while/body/eval_jaxpr/bhd,sd->bhs/dot_general | solution.py:12
  211.8 22.0 %fusion.49 = bf16[512,8]{0,1:T(8,128)(2,1)S(1)} fusion(f32[512,8,4096]{2,0,1:T(8,128)} %get-tuple-element.225, f32[512,8]{0,1:T(8,128)S(1)} %get-tuple-element.226, pred[4096]{0:T(1024)(128)(4,1)S(1)} %add_compare_fusion.2), kind=kLoop, calls=%fused_computation.8.clone.1 | loop fusion | flops 83881984 | bytes 67137536 | tf_op jit(solution)/shard_map/while/body/eval_jaxpr/reduce_sum | solution.py:18
  233.9 25.1 %fusion.48 = bf16[512,8,128]{0,2,1:T(8,128)(2,1)S(1)} fusion(f32[512,8,4096]{2,0,1:T(8,128)} %get-tuple-element.225, f32[512,8]{0,1:T(8,128)S(1)} %get-tuple-element.226, pred[4096]{0:T(1024)(128)(4,1)S(1)} %add_compare_fusion.2, bf16[4096,128]{0,1:T(8,128)(2,1)} %get-tuple-element.253), kind=kOutput, calls=%fused_computation.12.clone.1 | convolution fusion | flops 4379377664 | bytes 69226496 | tf_op jit(solution)/shard_map/while/body/eval_jaxpr/bhs,sd->bhd/dot_general | solution.py:19
  259.0 0.5 copy.128
  259.5 1.0 constant_dynamic-update-slice_fusion.2
  260.6 0.1 convert_element_type.44
  260.7 0.7 reshape.279
  261.4 11.0 %all-to-all-start.1 = ((bf16[8,2,512]{2,1,0:T(2,128)(2,1)}), bf16[8,2,512]{2,1,0:T(2,128)(2,1)S(1)}, u32[]{:S(2)}, u32[]{:S(2)}) async-start(bf16[8,2,512]{2,1,0:T(2,128)(2,1)} %reshape.279), calls=%async_computation.1 | async-start | bytes 32768 | tf_op jit(solution)/shard_map/all_to_all | solution.py:58
  272.5 0.1 convert_element_type.49
  272.6 0.1 reshape.281
  272.7 6.5 %all-to-all-done.1 = bf16[8,2,512]{2,1,0:T(2,128)(2,1)S(1)} async-done(((bf16[8,2,512]{2,1,0:T(2,128)(2,1)}), bf16[8,2,512]{2,1,0:T(2,128)(2,1)S(1)}, u32[]{:S(2)}, u32[]{:S(2)}) %all-to-all-start.1) | async-done | bytes 16416 | tf_op jit(solution)/shard_map/all_to_all | solution.py:58
  279.2 8.9 %all_to_all.20 = bf16[8,2,512]{2,1,0:T(2,128)(2,1)S(1)} all-to-all(bf16[8,2,512]{2,1,0:T(2,128)(2,1)S(1)} %reshape.281), channel_id=1, replica_groups=mesh['ctx'=8,'kvh'=4] {'ctx'}, dimensions={0} | all-to-all | bytes 32768 | tf_op jit(solution)/shard_map/all_to_all | solution.py:61
  288.1 4.5 %all-to-all-start.2 = ((bf16[8,2,64,1024]{3,2,1,0:T(8,128)(2,1)}), bf16[8,2,64,1024]{3,2,1,0:T(8,128)(2,1)}, u32[]{:S(2)}, u32[]{:S(2)}) async-start(bf16[8,2,64,1024]{3,2,1,0:T(8,128)(2,1)} %bitcast.123), calls=%async_computation.2 | async-start | bytes 4194304 | tf_op jit(solution)/shard_map/all_to_all | solution.py:57
  292.6 0.2 reduce-scatter.2.cloned.1.call-start
  292.9 0.1 copy.92
  293.0 0.1 reshape.247
  293.1 0.3 copy.109
  293.4 0.2 copy-done.7
  293.5 0.9 fusion.17
  294.4 0.1 copy.94
  294.6 1.5 fusion.18
  296.0 0.1 copy.98
  296.1 0.1 reshape.280
  296.3 0.1 reshape.282
  296.4 0.6 gather_fusion.1
  297.0 0.6 gather_fusion.3
  297.7 0.1 copy.102
  297.8 0.8 copy.95
  298.6 0.2 copy.96
  298.8 40.0 %all-to-all-done.2 = bf16[8,2,64,1024]{3,2,1,0:T(8,128)(2,1)} async-done(((bf16[8,2,64,1024]{3,2,1,0:T(8,128)(2,1)}), bf16[8,2,64,1024]{3,2,1,0:T(8,128)(2,1)}, u32[]{:S(2)}, u32[]{:S(2)}) %all-to-all-start.2) | async-done | bytes 2097184 | tf_op jit(solution)/shard_map/all_to_all | solution.py:57
  338.9 2.3 gather_fusion.2
  341.1 0.6 copy.111
  341.8 3.0 multiply_reduce_fusion
  344.8 2.0 divide_convert_fusion
  346.8 16.8 %convolution_convert_fusion = bf16[512,8192]{1,0:T(8,128)(2,1)} fusion(bf16[1024,8192]{1,0:T(8,128)(2,1)} %all-gather.2.cloned.1.call-done, bf16[64,8,8,128]{3,2,1,0:T(8,128)(2,1)S(1)} %bitcast.125), kind=kOutput, calls=%fused_computation.25 | convolution fusion | flops 8594128896 | bytes 26214400 | tf_op jit(solution)/shard_map/dot_general | solution.py:128
  363.7 1.3 broadcast_in_dim_reshape.3
  365.0 69.4 %reduce-scatter.2.cloned.1.call-done = bf16[512,2048]{1,0:T(8,128)(2,1)} async-done(((bf16[512,8192]{1,0:T(8,128)(2,1)}), bf16[512,2048]{1,0:T(8,128)(2,1)}) %reduce-scatter.2.cloned.1.call-update) | async-done | bytes 2097168 | tf_op jit(solution)/shard_map/reduce_scatter | solution.py:133
  (50 shorter events, 0.5 us)
Async XLA Ops:
  7.2 337.6 %copy-start = (bf16[8,64,1,128]{3,1,2,0:T(8,128)(2,1)S(1)}, bf16[8,64,1,128]{3,1,2,0:T(8,128)(2,1)}, u32[]{:S(2)}) copy-start(bf16[8,64,1,128]{3,1,2,0:T(8,128)(2,1)} %param.12) | copy-start | bytes 393220
  8.7 0.5 copy-start.9
  13.0 94.6 %all-to-all-start = ((bf16[8,2,64,1024]{3,2,1,0:T(8,128)(2,1)}), bf16[8,2,64,1024]{3,2,1,0:T(8,128)(2,1)S(1)}, u32[]{:S(2)}, u32[]{:S(2)}) async-start(bf16[8,2,64,1024]{3,2,1,0:T(8,128)(2,1)} %broadcast_select_fusion), calls=%async_computation | async-start | bytes 4194304 | tf_op jit(solution)/shard_map/all_to_all | solution.py:99
  20.2 1.2 copy-start.5
  20.2 2.5 copy-start.11
  20.3 326.6 %all-gather.2.cloned.1.call-start = ((), (), s32[]{:S(2)}) async-start(), calls=%async_computation.5 | async-start | bytes 18874368 | tf_op jit(solution)/shard_map/all_gather | solution.py:130
  107.6 2.0 copy-start.1
  261.4 17.8 %all-to-all-start.1 = ((bf16[8,2,512]{2,1,0:T(2,128)(2,1)}), bf16[8,2,512]{2,1,0:T(2,128)(2,1)S(1)}, u32[]{:S(2)}, u32[]{:S(2)}) async-start(bf16[8,2,512]{2,1,0:T(2,128)(2,1)} %reshape.279), calls=%async_computation.1 | async-start | bytes 32768 | tf_op jit(solution)/shard_map/all_to_all | solution.py:58
  288.1 4.7 %copy-start.8 = (s32[8]{0:T(128)S(1)}, s32[8]{0:T(128)}, u32[]{:S(2)}) copy-start(s32[8]{0:T(128)} %get-tuple-element.161) | copy-start | bytes 100
  288.1 4.7 %copy-start.10 = (s32[8]{0:T(128)S(1)}, s32[8]{0:T(128)}, u32[]{:S(2)}) copy-start(s32[8]{0:T(128)} %copy-done.9) | copy-start | bytes 100
  288.1 4.9 %copy-start.2 = (bf16[8,64,1,1024]{3,1,2,0:T(8,128)(2,1)S(1)}, bf16[8,64,1,1024]{3,1,2,0:T(8,128)(2,1)}, u32[]{:S(2)}) copy-start(bf16[8,64,1,1024]{3,1,2,0:T(8,128)(2,1)} %param.10) | copy-start | bytes 3145732
  288.1 50.7 %all-to-all-start.2 = ((bf16[8,2,64,1024]{3,2,1,0:T(8,128)(2,1)}), bf16[8,2,64,1024]{3,2,1,0:T(8,128)(2,1)}, u32[]{:S(2)}, u32[]{:S(2)}) async-start(bf16[8,2,64,1024]{3,2,1,0:T(8,128)(2,1)} %bitcast.123), calls=%async_computation.2 | async-start | bytes 4194304 | tf_op jit(solution)/shard_map/all_to_all | solution.py:57
  292.6 0.9 copy-start.7
  292.6 141.7 %reduce-scatter.2.cloned.1.call-start = ((), (), s32[]{:S(2)}) async-start(), calls=%async_computation.6 | async-start | bytes 10485760 | tf_op jit(solution)/shard_map/reduce_scatter | solution.py:133
  294.4 2.5 copy-start.3
  341.7 3.0 copy-start.4
  341.8 3.0 copy-start.6
Sparse Core Ops, SparseCore 0:
  23.3 258.8 all-gather.1
  363.8 70.5 reduce-scatter.1
where the time goes:
time: 442 us; the launch traced here: 441 us
  waiting for transfers between devices  201 us (45%)
  matrix products  117 us (26%)
  other arithmetic  55.4 us (13%)
  starting transfers between devices  23 us (5%)
  local copies, waits for them, and re-layouts  21 us (5%)
  between operations  14.4 us (3%)
  blocking collectives  8.93 us (2%)
    all_to_all x1, waiting for transfers between devices, local(): lax.all_to_all(outgoing, 'ctx', split_axis=0, concat_axis=0, tiled=True)  84.2 us
    reduce_scatter x1, waiting for transfers between devices, local(): lax.psum_scatter(partial_terms.astype(jnp.bfloat16), 'kvh', scatter_dimen...  69.4 us
    dot_general x3, matrix products, partial_block(): jnp.einsum('bhs,sd->bhd', weights.astype(jnp.bfloat16), shard_values, pre...  52 us
    dot_general x3, matrix products, partial_block(): jnp.einsum('bhd,sd->bhs', query_rows, shard_keys, preferred_element_type=...  48.7 us
    reduce_sum x3, other arithmetic, partial_block(): totals = jnp.sum(weights, axis=-1)  47.5 us
    all_to_all x1, waiting for transfers between devices, return_partials(): lax.all_to_all(parts[0], 'ctx', split_axis=0, concat_axis=0, tiled=True)  40 us
    dot_general x1, matrix products, local(): jnp.dot(flat_rows, lax.all_gather(out_weight, 'ctx', axis=1, tiled=True),...  16.8 us
    all_to_all x1, starting transfers between devices, return_partials(): lax.all_to_all(parts[1].astype(jnp.bfloat16), 'ctx', split_axis=0, concat...  11 us
  transfers between devices with their start and end apart: 5, of which 4 were waited for; matrix products, arithmetic and copies ran while one was open for 39% of the time, Pallas kernels for 0%

commit v1 on v0

v1 whole, which is shorter than its diff:
```python
import functools
import math

import jax
import jax.numpy as jnp
from jax import lax
from jax.experimental import pallas as pl
from jax.experimental.pallas import tpu as pltpu
from jax.sharding import PartitionSpec as P

MASKED = -1e30
LOG2E = math.log2(math.e)
LANES = 128
PART_ROWS = 16
MAX_TILE = 1024
MAX_BLOCK = 512


def nt_dot(a, b):
    return lax.dot_general(a, b, (((1,), (1,)), ((), ())), preferred_element_type=jnp.float32)


def after(x, *others):
    return lax.optimization_barrier((x, *others))[0]


def pack_kernel(capacity, holders, slots, prompt_ref, len_ref, q_ref, *refs):
    *chunk_refs, meta_ref = refs
    responses, tokens, _ = q_ref.shape
    position = lax.axis_index("ctx")
    mine, holder = position // holders, position % holders
    named = [prompt_ref[position * responses + r] for r in range(responses)]
    ranks = []
    for r in range(responses):
        rank = jnp.int32(0)
        for before in range(r):
            rank += (named[before] == named[r]).astype(jnp.int32)
        ranks.append(rank)
    places = len(chunk_refs) * capacity
    for i, chunk_ref in enumerate(chunk_refs):
        for slot in range(capacity):
            chosen, present = jnp.int32(0), jnp.int32(0)
            for r in range(responses):
                hit = ((named[r] == mine ^ i) & (ranks[r] == slot)).astype(jnp.int32)
                chosen += hit * r
                present += hit
            meta_ref[i * capacity + slot] = chosen
            meta_ref[places + i * capacity + slot] = present
            rows = slice(slot * tokens, (slot + 1) * tokens)
            chunk_ref[rows, :] = q_ref[chosen]

            @pl.when(present == 0)
            def _(chunk_ref=chunk_ref, rows=rows):
                chunk_ref[rows, :] = jnp.zeros_like(chunk_ref[rows, :])

    length = len_ref[mine]
    for j in range(holders):
        place = (holder + j) % holders
        meta_ref[2 * places + j] = jnp.clip(length - place * slots, 0, slots)
        meta_ref[2 * places + holders + j] = place


def pack(prompt_of, prefix_len, q, capacity, holders, slots):
    _, tokens, width = q.shape
    prompts = prefix_len.shape[0]
    smem = pl.BlockSpec(memory_space=pltpu.SMEM)
    vmem = pl.BlockSpec(memory_space=pltpu.VMEM)
    *chunks, meta = pl.pallas_call(
        functools.partial(pack_kernel, capacity, holders, slots),
        out_shape=[jax.ShapeDtypeStruct((capacity * tokens, width), q.dtype)] * prompts
        + [jax.ShapeDtypeStruct((2 * (prompts * capacity + holders),), jnp.int32)],
        in_specs=[smem, smem, vmem],
        out_specs=[vmem] * prompts + [smem],
        cost_estimate=pl.CostEstimate(flops=0, bytes_accessed=4 * q.size, transcendentals=0),
        name="pack",
    )(prompt_of, prefix_len, q)
    return chunks, meta


def attend_kernel(count, first, last, shard, places, meta_ref, *refs):
    q_refs, (k_ref, v_ref, *refs) = refs[:count], refs[count:]
    if not first:
        prev_o_ref, prev_lse_ref, *refs = refs
    if last:
        out_refs, refs = refs[:count], refs[count:]
    else:
        o_ref, lse_ref, *refs = refs
    qext, kext, vext, score_a, score_b = refs
    tokens = q_refs[0].shape[0]
    slots, hd = k_ref.shape
    heads = q_refs[0].shape[1] // hd
    scale = LOG2E / math.sqrt(hd)
    tiles, row_block, key_tile = score_a.shape
    per_chunk = heads * tokens // row_block
    live = meta_ref[2 * places + shard]

    @pl.when(live == slots)
    def _():
        for t in range(tiles):
            at = slice(t * key_tile, (t + 1) * key_tile)
            keys = k_ref[at, :]
            kext[at, :hd] = keys
            kext[at, hd:] = keys
            vext[at, :hd] = v_ref[at, :]
            vext[at, hd:] = jnp.ones((key_tile, hd), jnp.bfloat16)

    @pl.when(live != slots)
    def _():
        def prepare(step, carry):
            at = pl.ds(pl.multiple_of(step * key_tile, key_tile), key_tile)
            alive = step * key_tile + lax.broadcasted_iota(jnp.int32, (key_tile, hd), 0) < live
            keys = jnp.where(alive, k_ref[at, :].astype(jnp.float32), k_ref[0:1, :].astype(jnp.float32))
            keys = keys.astype(jnp.bfloat16)
            kext[at, :hd] = keys
            kext[at, hd:] = keys
            vext[at, :hd] = jnp.where(alive, v_ref[at, :].astype(jnp.float32), 0.0).astype(jnp.bfloat16)
            vext[at, hd:] = jnp.where(alive, 1.0, 0.0).astype(jnp.bfloat16)
            return carry

        lax.fori_loop(0, tiles, prepare, 0)

    for c, q_ref in enumerate(q_refs):
        for h in range(heads):
            rows = slice((c * heads + h) * tokens, (c * heads + h + 1) * tokens)
            x = q_ref[:, h * hd : (h + 1) * hd].astype(jnp.float32) * scale
            high = x.astype(jnp.bfloat16)
            qext[rows, :hd] = high
            qext[rows, hd:] = (x - high.astype(jnp.float32)).astype(jnp.bfloat16)

    low = jnp.full((row_block, LANES), MASKED, jnp.float32)

    def rows_of(b):
        if isinstance(b, int):
            return slice(b * row_block, (b + 1) * row_block)
        return pl.ds(pl.multiple_of(b * row_block, row_block), row_block)

    def score_tile(b, t, into, peak):
        s = nt_dot(qext[rows_of(b), :], kext[t * key_tile : (t + 1) * key_tile, :])
        into[t] = s
        for j in range(key_tile // LANES):
            peak = jnp.maximum(peak, s[:, j * LANES : (j + 1) * LANES])
        return peak

    def one_block(b, scores, peak, following, into):
        m = jnp.max(peak, axis=1, keepdims=True)
        peak = low
        acc = jnp.zeros((row_block, 2 * hd), jnp.float32)
        for t in range(tiles):
            if following is not None:
                peak = score_tile(following, t, into, peak)
            w = jnp.exp2(scores[t] - m).astype(jnp.bfloat16)
            acc = acc + jnp.dot(
                w, vext[t * key_tile : (t + 1) * key_tile, :], preferred_element_type=jnp.float32
            )
        total = acc[:, hd:]
        some = total > 0.0
        safe = jnp.where(some, total, 1.0)
        o = acc[:, :hd] / safe
        lse = jnp.where(some, m + jnp.log2(safe), MASKED)
        rows = rows_of(b)
        if not first:
            before = prev_lse_ref[rows, :]
            top = jnp.maximum(before, lse)
            w_before = jnp.exp2(before - top)
            w_now = jnp.exp2(lse - top)
            both = w_before + w_now
            o = (w_before * prev_o_ref[rows, :] + w_now * o) / both
            lse = top + jnp.log2(both)
        if not last:
            o_ref[rows, :] = o
            lse_ref[rows, :] = lse
            return peak
        out_ref = out_refs[b // per_chunk]
        for j in range(row_block // tokens):
            h = (b % per_chunk) * (row_block // tokens) + j
            part = slice(j * tokens, (j + 1) * tokens)
            lanes = slice(h * hd, (h + 1) * hd)
            out_ref[:tokens, lanes] = o[part].astype(jnp.bfloat16)
            flat = lse[part].T[:PART_ROWS, :]
            high = flat.astype(jnp.bfloat16).astype(jnp.float32)
            middle = (flat - high).astype(jnp.bfloat16).astype(jnp.float32)
            row = lax.broadcasted_iota(jnp.int32, flat.shape, 0)
            out_ref[tokens:, lanes] = jnp.where(
                row == 0, high, jnp.where(row == 1, middle, jnp.where(row == 2, flat - high - middle, 0.0))
            ).astype(jnp.bfloat16)
        return peak

    blocks = count * per_chunk
    peak = low
    for t in range(tiles):
        peak = score_tile(0, t, score_a, peak)
    looped = 0
    if not last and per_chunk == 2 and count > 1:
        looped = blocks - 2

        def pair(i, peak):
            peak = one_block(2 * i, score_a, peak, 2 * i + 1, score_b)
            return one_block(2 * i + 1, score_b, peak, 2 * i + 2, score_a)

        peak = lax.fori_loop(0, looped // 2, pair, peak)
    for b in range(looped, blocks):
        scores, into = (score_a, score_b) if b % 2 == 0 else (score_b, score_a)
        peak = one_block(b, scores, peak, b + 1 if b + 1 < blocks else None, into)


def attend(meta, places, queries, keys, values, slots, shard, state, state_block, last):
    count = len(queries)
    tokens, width = queries[0].shape
    whole = keys.shape[0] > slots
    hd = keys.shape[1] // 2 if whole else keys.shape[1]
    rows = tokens * (width // hd)
    row_block = min(MAX_BLOCK, rows)
    key_tile = min(MAX_TILE, slots)
    holders = meta.shape[0] // 2 - places
    first = state is None

    def fixed(shape):
        return pl.BlockSpec(shape, lambda i, meta_ref: (0, 0))

    def shard_at(column):
        if not whole:
            return pl.BlockSpec((slots, hd), lambda i, meta_ref: (0, 0))
        return pl.BlockSpec(
            (slots, hd), lambda i, meta_ref: (meta_ref[2 * places + holders + shard], column)
        )

    in_specs = [fixed((tokens, width))] * count + [shard_at(0), shard_at(1)]
    operands = [meta, *queries, keys, values]
    if not first:
        in_specs += [pl.BlockSpec((count * rows, hd), lambda i, meta_ref: (state_block, 0))] * 2
        operands += state
    if last:
        out_shape = [jax.ShapeDtypeStruct((tokens + PART_ROWS, width), jnp.bfloat16)] * count
        out_specs = [fixed((tokens + PART_ROWS, width))] * count
    else:
        out_shape = [jax.ShapeDtypeStruct((count * rows, hd), jnp.float32)] * 2
        out_specs = [fixed((count * rows, hd))] * 2
    return pl.pallas_call(
        functools.partial(attend_kernel, count, first, last, shard, places),
        grid_spec=pltpu.PrefetchScalarGridSpec(
            num_scalar_prefetch=1,
            grid=(1,),
            in_specs=in_specs,
            out_specs=out_specs,
            scratch_shapes=[
                pltpu.VMEM((count * rows, 2 * hd), jnp.bfloat16),
                pltpu.VMEM((slots, 2 * hd), jnp.bfloat16),
                pltpu.VMEM((slots, 2 * hd), jnp.bfloat16),
                pltpu.VMEM((slots // key_tile, row_block, key_tile), jnp.float32),
                pltpu.VMEM((slots // key_tile, row_block, key_tile), jnp.float32),
            ],
        ),
        out_shape=out_shape,
        compiler_params=pltpu.CompilerParams(vmem_limit_bytes=50 * 1024 * 1024),
        cost_estimate=pl.CostEstimate(
            flops=4 * count * rows * slots * hd,
            bytes_accessed=4 * slots * hd,
            transcendentals=count * rows * slots,
        ),
        name="attend_last" if last else "attend",
    )(*operands)


def combine_kernel(capacity, meta_ref, q_ref, k_ref, v_ref, *refs):
    *part_refs, out_ref, stacked = refs
    _, tokens, hd = k_ref.shape
    width = q_ref.shape[2]
    heads = width // hd
    scale = LOG2E / math.sqrt(hd)
    places = len(part_refs) * capacity
    for i, part_ref in enumerate(part_refs):
        for slot in range(capacity):
            r = meta_ref[i * capacity + slot]

            @pl.when(meta_ref[places + i * capacity + slot] > 0)
            def _(r=r, part_ref=part_ref, slot=slot):
                for h in range(heads):
                    stacked[h * tokens : (h + 1) * tokens, :] = q_ref[r, :, h * hd : (h + 1) * hd]
                s = nt_dot(stacked[...], k_ref[r]) * scale
                row = lax.broadcasted_iota(jnp.int32, s.shape, 0) % tokens
                seen = row >= lax.broadcasted_iota(jnp.int32, s.shape, 1)
                s = jnp.where(seen, s, MASKED)
                m = jnp.max(s, axis=1, keepdims=True)
                w = jnp.where(seen, jnp.exp2(s - m), 0.0)
                total = jnp.sum(w, axis=1, keepdims=True)
                o = jnp.dot(w.astype(jnp.bfloat16), v_ref[r], preferred_element_type=jnp.float32)
                base = part_ref.shape[0] - PART_ROWS
                for h in range(heads):
                    rows = slice(h * tokens, (h + 1) * tokens)
                    lanes = slice(h * hd, (h + 1) * hd)
                    far = part_ref[slot * tokens : (slot + 1) * tokens, lanes].astype(jnp.float32)
                    pieces = part_ref[base:, lanes].astype(jnp.float32)
                    flat = pieces[0:1] + pieces[1:2] + pieces[2:3]
                    lse = jnp.broadcast_to(flat, (hd, hd)).T[slot * tokens : (slot + 1) * tokens, :]
                    top = jnp.maximum(m[rows], lse)
                    own_scale = jnp.exp2(m[rows] - top)
                    far_scale = jnp.exp2(lse - top)
                    out_ref[r, :, lanes] = (
                        (own_scale * o[rows] + far_scale * far) / (own_scale * total[rows] + far_scale)
                    ).astype(jnp.bfloat16)


def combine(meta, capacity, q, keys, values, parts):
    responses, tokens, width = q.shape
    hd = keys.shape[-1]
    heads = width // hd
    return pl.pallas_call(
        functools.partial(combine_kernel, capacity),
        out_shape=jax.ShapeDtypeStruct(q.shape, jnp.bfloat16),
        in_specs=[pl.BlockSpec(memory_space=pltpu.SMEM)]
        + [pl.BlockSpec(memory_space=pltpu.VMEM)] * (3 + len(parts)),
        out_specs=pl.BlockSpec(memory_space=pltpu.VMEM),
        scratch_shapes=[pltpu.VMEM((heads * tokens, hd), jnp.bfloat16)],
        compiler_params=pltpu.CompilerParams(vmem_limit_bytes=24 * 1024 * 1024),
        cost_estimate=pl.CostEstimate(
            flops=4 * responses * heads * tokens * tokens * hd,
            bytes_accessed=8 * responses * tokens * width,
            transcendentals=responses * heads * tokens * tokens,
        ),
        name="combine",
    )(meta, q, keys, values, *parts)


INWARD = ((0, 2), (3, 1))
OUTWARD = ((1, 0), (2, 3))


def plane_hop(x, pairs):
    return lax.ppermute(x, "ctx", [(a * 2 + h, b * 2 + h) for a, b in pairs for h in range(2)])


def project(rows, other, blocks, plane, holder):
    group = lax.axis_index("kvh")
    groups = lax.axis_size("kvh")
    count = rows.shape[0]
    apart = plane ^ group
    even = apart & 1 == 0
    low = apart < 2
    block0, block1, block3, two_in, out_a, out_b = blocks
    half = out_a.shape[1]
    inner = (plane == 1) | (plane == 2)

    def swap_holders(x, keep):
        pairs = [
            ((p * 2 + h) * groups + k, (p * 2 + 1 - h) * groups + k)
            for p in range(groups)
            for h in range(2)
            for k in range(groups)
            if keep(p ^ k)
        ]
        return lax.ppermute(x, ("ctx", "kvh"), pairs)

    def to_group(x, flip, keep):
        pairs = [
            (c * groups + (k ^ flip), c * groups + k)
            for c in range(2 * groups)
            for k in range(groups)
            if keep(c // 2 ^ k)
        ]
        return lax.ppermute(x, ("ctx", "kvh"), pairs)

    def terms(x, block):
        return jnp.dot(x, block, preferred_element_type=jnp.float32).astype(jnp.bfloat16)

    def add(a, b):
        return (a.astype(jnp.float32) + b.astype(jnp.float32)).astype(jnp.bfloat16)

    def pair_sums(x):
        term0, term1, term3 = terms(x, block0), terms(x, block1), terms(x, block3)
        sent = jnp.concatenate([jnp.where(even, term1, term0), term3], axis=1)
        got = to_group(sent, 1, lambda i: True)
        width = term0.shape[1]
        return add(jnp.where(even, term0, term1), got[:, :width]), add(term3, got[:, width:])

    def chip_sums(near, far):
        got = to_group(jnp.where(low, far, near), 2, lambda i: i != 2)
        return add(jnp.where(low, near, far), got)

    mine_sums = pair_sums(rows)
    mine = chip_sums(*mine_sums)
    other, out_a, *mine_sums = lax.optimization_barrier((other, out_a, *mine_sums))
    their_sums = pair_sums(other)
    theirs = chip_sums(*their_sums)
    both = jnp.concatenate([rows, other], axis=0)

    def last_block(came_in, came_out, *ready):
        came_out = after(came_out, *ready)
        term = terms(both, jnp.where(inner, came_in, came_out))
        return add(term, to_group(term, 1, lambda i: i & 1 == 0))

    def last_sums(total):
        total = add(total, to_group(total, 2, lambda i: i == 2))
        return total[:count], swap_holders(total[count:], lambda i: i == 2)

    half_a = last_block(two_in[:, :half], out_a, *their_sums, mine)
    half_b = last_block(two_in[:, half:], out_b, half_a)
    half_b = after(half_b, theirs)
    back = swap_holders(theirs, lambda i: i != 2)
    mine_a, back_a = last_sums(half_a)
    mine_b, back_b = last_sums(half_b)
    mine = jnp.where(apart == 2, jnp.concatenate([mine_a, mine_b], axis=1), mine)
    back = jnp.where(apart == 2, jnp.concatenate([back_a, back_b], axis=1), back)
    return jnp.where(
        holder == 0,
        jnp.concatenate([mine, back], axis=1),
        jnp.concatenate([back, mine], axis=1),
    )


def local(
    queries, resp_keys, resp_values, prefix_keys, prefix_values, prefix_len, prompt_of, out_weight
):
    ctx_count = lax.axis_size("ctx")
    kvh_count = lax.axis_size("kvh")
    position = lax.axis_index("ctx")
    own_queries = queries[:, :, 0]
    own_keys = resp_keys[:, :, 0]
    own_values = resp_values[:, :, 0]
    resp_count, tokens_each, width = own_queries.shape
    slot_count = prefix_keys.shape[0]
    prompts = prefix_len.shape[0]
    holders = ctx_count // prompts
    my_prompt = position // holders
    my_holder = position % holders
    capacity = max(LANES // tokens_each, resp_count // prompts)
    places = prompts * capacity
    by_plane = kvh_count == prompts == 4 and holders == 2

    def cross(x, i):
        pairs = [(p * holders + h, (p ^ i) * holders + h) for p in range(prompts) for h in range(holders)]
        return lax.ppermute(x, "ctx", pairs)

    if by_plane:
        one, three = cross(out_weight, 1), cross(out_weight, 3)
        two_in = plane_hop(out_weight, INWARD)
    chunks, meta = pack(prompt_of, prefix_len, own_queries, capacity, holders, slot_count)
    chunks = chunks[:1] + [cross(x, i) for i, x in enumerate(chunks) if i > 0]
    near = prefix_keys[:, 0], prefix_values[:, 0]
    lines = [[p * holders + h for h in range(holders)] for p in range(prompts)]
    joined = jnp.concatenate(near, axis=1)
    joined = lax.all_gather(joined, "ctx", axis=0, tiled=True, axis_index_groups=lines)
    far = joined, joined
    away = chunks[:0:-1]

    state_home = state_away = None
    for shard in range(holders - 1):
        kv = near if shard == 0 else far
        state_home = attend(meta, places, chunks[:1], *kv, slot_count, shard, state_home, 0, False)
        state_home, away = lax.optimization_barrier((state_home, away))
        state_away = attend(meta, places, away, *kv, slot_count, shard, state_away, 0, False)
    shard = holders - 1
    done = [None] * prompts
    for where, members in enumerate([range(prompts - 1, 1, -1), [1]]):
        queries_now = [away[prompts - 1 - i] for i in members]
        block = 0 if where == 0 else prompts - 2
        results = attend(meta, places, queries_now, *far, slot_count, shard, state_away, block, True)
        for i, x in zip(members, results):
            done[i] = cross(x, i)
        if by_plane and where == 0:
            one, three, state_away = lax.optimization_barrier((one, three, state_away))
            half = out_weight.shape[1] // 2
            two_out = [plane_hop(x, OUTWARD) for x in (three[:, :half], three[:, half:])]
    if by_plane:
        two_in, state_home = lax.optimization_barrier((two_in, state_home))
    (done[0],) = attend(meta, places, chunks[:1], *far, slot_count, shard, state_home, 0, True)
    attended = combine(meta, capacity, own_queries, own_keys, own_values, done)
    rows = attended.reshape(resp_count * tokens_each, width)

    if by_plane:
        other = lax.ppermute(
            rows, "ctx", [(p * 2 + h, p * 2 + 1 - h) for p in range(prompts) for h in range(2)]
        )
        blocks = out_weight, one, three, two_in, *two_out
        projected = project(rows, other, blocks, my_prompt, my_holder)
    else:
        weights = lax.all_gather(out_weight, "ctx", axis=1, tiled=True)
        terms = jnp.dot(rows, weights, preferred_element_type=jnp.float32)
        projected = lax.psum_scatter(
            terms.astype(jnp.bfloat16), "kvh", scatter_dimension=1, tiled=True
        )
    return (attended[:, :, None, :], projected)


def solution(mesh):
    in_specs = (
        P("ctx", None, "kvh", None),
        P("ctx", None, "kvh", None),
        P("ctx", None, "kvh", None),
        P("ctx", "kvh", None),
        P("ctx", "kvh", None),
        P(),
        P(),
        P("kvh", "ctx"),
    )
    out_specs = (P("ctx", None, "kvh", None), P("ctx", "kvh"))
    return jax.shard_map(local, mesh=mesh, in_specs=in_specs, out_specs=out_specs, check_vma=False)
```

time: 442 us -> 427 us (0.966)
  the two profiles are of different devices: /device:TPU:0 before, /device:TPU:6 now
where the time goes in v1:
time: 427 us; the launch traced here: 420 us
  waiting for transfers between devices  235 us (55%)
  Pallas kernels  62.3 us (15%)
  starting transfers between devices  48.6 us (11%)
  matrix products  27.4 us (6%)
  other arithmetic  21.1 us (5%)
  between operations  14.9 us (3%)
  local copies, waits for them, and re-layouts  11.1 us (3%)
    ppermute x8, waiting for transfers between devices, cross(): return lax.ppermute(x, 'ctx', pairs)  143 us
    pallas_call x5, Pallas kernels, attend(): pl.pallas_call(functools.partial(attend_kernel, count, first, last, shard...  54.3 us
    ppermute x3, waiting for transfers between devices, plane_hop(): lax.ppermute(x, 'ctx', [(a * 2 + h, b * 2 + h) for a, b in pairs for h in...  42.1 us
    ppermute x8, waiting for transfers between devices, to_group(): return lax.ppermute(x, ('ctx', 'kvh'), pairs)  41.3 us
    dot_general x8, matrix products, terms(): jnp.dot(x, block, preferred_element_type=jnp.float32).astype(jnp.bfloat16)  27.4 us
    ppermute x8, starting transfers between devices, cross(): return lax.ppermute(x, 'ctx', pairs)  22.2 us
    ppermute x8, starting transfers between devices, to_group(): return lax.ppermute(x, ('ctx', 'kvh'), pairs)  13.3 us
    ppermute x3, waiting for transfers between devices, swap_holders(): return lax.ppermute(x, ('ctx', 'kvh'), pairs)  8.6 us
  transfers between devices with their start and end apart: 24, of which 11 were waited for; matrix products, arithmetic and copies ran while one was open for 4% of the time, Pallas kernels for 14%

profile of v1, /device:TPU:6, one launch (start us, length us, event | category | flops | bytes accessed | tf_op | source)
XLA Modules:
  0.0 420.4 jit_solution(4987945661363248108)
XLA Ops:
  7.2 3.1 pad_maximum_fusion
  10.3 1.6 collective-permute-start.4
  12.0 2.5 collective-permute-start.5
  14.4 3.4 collective-permute-start
  17.8 2.6 pack.1
  20.4 3.0 collective-permute-start.1
  23.4 133.3 %collective-permute-done.1.refs_0_ = bf16[128,1024]{1,0:T(8,128)(2,1)S(1)} collective-permute-done((bf16[128,1024]{1,0:T(8,128)(2,1)}, bf16[128,1024]{1,0:T(8,128)(2,1)S(1)}, u32[]{:S(2)}, u32[]{:S(2)}) %collective-permute-start.1) | collective-permute-done | bytes 262176 | tf_op jit(solution)/shard_map/ppermute | solution.py:431
  156.7 11.8 %collective-permute-start.3 = (bf16[128,1024]{1,0:T(8,128)(2,1)}, bf16[128,1024]{1,0:T(8,128)(2,1)S(1)}, u32[]{:S(2)}, u32[]{:S(2)}) collective-permute-start(bf16[128,1024]{1,0:T(8,128)(2,1)} %get-tuple-element.36), channel_id=1, source_target_pairs={{0,8},{4,12},{8,0},{12,4},{16,24},{20,28},{24,16},{28,20},{1,9},{5... | collective-permute-start | bytes 786440 | tf_op jit(solution)/shard_map/ppermute | solution.py:431
  168.6 0.9 copy-done.6
  169.6 0.6 copy-done.10
  170.2 6.2 %attend.2 = (f32[1024,128]{1,0:T(8,128)S(1)}, f32[1024,128]{1,0:T(8,128)S(1)}) custom-call(s32[20]{0:T(128)S(1)} %copy-done.10, bf16[128,1024]{1,0:T(8,128)(2,1)S(1)} %copy-done.6, bf16[4096,128]{1,0:T(8,128)(2,1)S(1)} %bitcast.27, bf16[4096,128]{1,0:T(8,128)(2,1)S(1)} %bitcast.24), custom_call_target="tpu_custom_call" | custom-call | flops 2147483648 | bytes 2097152 | tf_op jit(solution)/shard_map/attend/pallas_call | solution.py:238
  176.4 1.5 collective-permute-done.3.refs_2_.refs_0_
  177.8 17.9 %attend.3 = (f32[3072,128]{1,0:T(8,128)}, f32[3072,128]{1,0:T(8,128)}) custom-call(s32[20]{0:T(128)S(1)} %copy-done.10, bf16[128,1024]{1,0:T(8,128)(2,1)S(1)} %collective-permute-done.1.refs_0_, bf16[128,1024]{1,0:T(8,128)(2,1)S(1)} %collective-permute-done.2.refs_1_, bf16[128,1024]{1,0:T(8,128)(2,1)S(1)} %collective-permute-done.3.refs_2_.refs_0_, ...), custom_call_target="tpu_custom_call" | custom-call | flops 6442450944 | bytes 2097152 | tf_op jit(solution)/shard_map/attend/pallas_call | solution.py:238
  195.8 1.4 copy-done.1
  197.2 0.9 copy-done.13
  198.1 0.9 copy-done.15
  199.1 13.9 %attend_last.5 = (bf16[144,1024]{1,0:T(8,128)(2,1)S(1)}, bf16[144,1024]{1,0:T(8,128)(2,1)S(1)}) custom-call(s32[20]{0:T(128)S(1)} %copy-done.11, bf16[128,1024]{1,0:T(8,128)(2,1)S(1)} %copy-done.13, bf16[128,1024]{1,0:T(8,128)(2,1)S(1)} %copy-done.15, bf16[8192,256]{1,0:T(8,128)(2,1)} %all-gather.2.cloned.1.call-done.refs_1_.refs_2_.refs_3_, ...), custom_call_target="tpu_custom_call" | custom-call | flops 4294967296 | bytes 2097152 | tf_op jit(solution)/shard_map/attend_last/pallas_call | solution.py:238
  213.2 2.2 collective-permute-start.8
  215.4 8.2 %attend_last.4 = bf16[144,1024]{1,0:T(8,128)(2,1)S(1)} custom-call(s32[20]{0:T(128)S(1)} %copy-done.11, bf16[128,1024]{1,0:T(8,128)(2,1)S(1)} %collective-permute-done.3.refs_2_.refs_0_, bf16[8192,256]{1,0:T(8,128)(2,1)} %all-gather.2.cloned.1.call-done.refs_1_.refs_2_.refs_3_, bf16[8192,256]{1,0:T(8,128)(2,1)} %all-gather.2.cloned.1.call-done.refs_1_.refs_2_.refs_3_, ...), custom_call_target="tpu_custom_call" | custom-call | flops 2147483648 | bytes 2097152 | tf_op jit(solution)/shard_map/attend_last/pallas_call | solution.py:238
  223.7 0.8 collective-permute-start.6
  224.5 8.1 %attend_last.3.refs_0_ = bf16[144,1024]{1,0:T(8,128)(2,1)S(1)} custom-call(s32[20]{0:T(128)S(1)} %copy-done.11, bf16[128,1024]{1,0:T(8,128)(2,1)S(1)} %copy-done.7, bf16[8192,256]{1,0:T(8,128)(2,1)} %all-gather.2.cloned.1.call-done.refs_1_.refs_2_.refs_3_, bf16[8192,256]{1,0:T(8,128)(2,1)} %all-gather.2.cloned.1.call-done.refs_1_.refs_2_.refs_3_, ...), custom_call_target="tpu_custom_call" | custom-call | flops 2147483648 | bytes 2097152 | tf_op jit(solution)/shard_map/attend_last/pallas_call | solution.py:238
  232.6 2.1 collective-permute-done.7.refs_2_
  234.7 6.2 %collective-permute-done.6.refs_1_ = bf16[144,1024]{1,0:T(8,128)(2,1)S(1)} collective-permute-done((bf16[144,1024]{1,0:T(8,128)(2,1)S(1)}, bf16[144,1024]{1,0:T(8,128)(2,1)S(1)}, u32[]{:S(2)}, u32[]{:S(2)}) %collective-permute-start.6) | collective-permute-done | bytes 294944 | tf_op jit(solution)/shard_map/ppermute | solution.py:431
  240.8 5.4 %combine.1 = bf16[8,64,1024]{2,1,0:T(8,128)(2,1)} custom-call(s32[20]{0:T(128)S(1)} %copy-done.11, bf16[8,64,1024]{2,1,0:T(8,128)(2,1)S(1)} %bitcast.22, bf16[8,64,128]{2,1,0:T(8,128)(2,1)S(1)} %bitcast.29, bf16[8,64,128]{2,1,0:T(8,128)(2,1)S(1)} %bitcast.30, bf16[144,1024]{1,0:T(8,128)(2,1)S(1)} %attend_last.3.refs_0_, ...), custom_call_target="tpu_custom_call" | custom-call | flops 134217728 | bytes 4194304 | tf_op jit(solution)/shard_map/combine/pallas_call | solution.py:307
  246.3 2.5 convolution_convert_fusion.7
  248.8 3.5 convolution_convert_fusion.5
  252.3 4.2 broadcast_select_fusion.3
  256.5 1.5 pad_maximum_fusion.1
  258.0 3.1 fusion.8
  261.1 1.3 collective-permute-start.10
  262.4 0.6 collective-permute-start.9
  263.0 1.3 copy-done.18
  264.3 4.4 %broadcast_select_fusion.1 = (bf16[512,1024]{1,0:T(8,128)(2,1)}, bf16[512,1024]{1,0:T(8,128)(2,1)S(1)}, bf16[512,1024]{1,0:T(8,128)(2,1)S(1)}) fusion(pred[]{:T(512)S(6)} %lt.10, bf16[512,2048]{1,0:T(8,128)(2,1)} %copy-done.18, bf16[512,1024]{1,0:T(8,128)(2,1)S(1)} %convolution_convert_fusion.5, bf16[512,1024]{1,0:T(8,128)(2,1)} %copy-done.22, ...), kind=kLoop, calls=%fused_computation.30 | loop fusion | flops 5242880 | bytes 8388610 | tf_op jit(solution)/shard_map/jit(_where)/select_n | solution.py:376
  268.7 20.1 %collective-permute-done.10 = bf16[1024,512]{1,0:T(8,128)(2,1)} collective-permute-done((bf16[1024,512]{1,0:T(8,128)(2,1)}, bf16[1024,512]{1,0:T(8,128)(2,1)}, u32[]{:S(2)}, u32[]{:S(2)}) %collective-permute-start.10) | collective-permute-done | bytes 1048608 | tf_op jit(solution)/shard_map/ppermute | solution.py:329
  288.9 2.5 convolution_convert_fusion.4
  291.3 3.5 convolution_convert_fusion.2
  294.9 4.5 %broadcast_select_fusion.2 = (bf16[512,1024]{1,0:T(8,128)(2,1)S(1)}, bf16[512,1024]{1,0:T(8,128)(2,1)}) fusion(bf16[512,1024]{1,0:T(8,128)(2,1)S(1)} %convolution_convert_fusion.4, pred[]{:T(512)S(6)} %eq.20, bf16[512,1024]{1,0:T(8,128)(2,1)} %collective-permute-done.9, bf16[1024,1024]{1,0:T(8,128)(2,1)} %collective-permute-done.4), kind=kOutput, calls=%fused_computation.33 | convolution fusion | flops 1074790400 | bytes 6291457 | tf_op jit(solution)/shard_map/dot_general | solution.py:363
  299.4 1.5 pad_maximum_fusion.3
  301.0 3.6 collective-permute-start.13
  304.7 22.1 %collective-permute-done.13 = bf16[512,1024]{1,0:T(8,128)(2,1)} collective-permute-done((bf16[512,1024]{1,0:T(8,128)(2,1)}, bf16[512,1024]{1,0:T(8,128)(2,1)}, u32[]{:S(2)}, u32[]{:S(2)}) %collective-permute-start.13) | collective-permute-done | bytes 1048608 | tf_op jit(solution)/shard_map/ppermute | solution.py:360
  326.8 1.9 add_convert_fusion.5
  328.7 2.9 broadcast_select_fusion
  331.6 3.5 convolution_convert_fusion.1
  335.2 1.3 collective-permute-start.14
  336.5 1.3 collective-permute-start.16
  337.8 4.5 %collective-permute-start.18 = (bf16[512,1024]{1,0:T(8,128)(2,1)S(1)}, bf16[512,1024]{1,0:T(8,128)(2,1)S(1)}, u32[]{:S(2)}, u32[]{:S(2)}) collective-permute-start(bf16[512,1024]{1,0:T(8,128)(2,1)S(1)} %get-tuple-element.63), channel_id=1, source_target_pairs={{2,0},{3,1},{1,3},{6,4},{7,5},{5,7},{10,8},{11,9},{8,10},{14,12},{... | collective-permute-start | bytes 3145736 | tf_op jit(solution)/shard_map/ppermute | solution.py:360
  342.5 22.0 %collective-permute-done.16 = bf16[1024,512]{1,0:T(8,128)(2,1)S(1)} collective-permute-done((bf16[1024,512]{1,0:T(8,128)(2,1)S(1)}, bf16[1024,512]{1,0:T(8,128)(2,1)S(1)}, u32[]{:S(2)}, u32[]{:S(2)}) %collective-permute-start.16) | collective-permute-done | bytes 1048608 | tf_op jit(solution)/shard_map/ppermute | solution.py:329
  364.6 3.1 convolution_convert_fusion
  367.7 1.3 collective-permute-start.17
  369.0 1.3 collective-permute-start.15
  370.3 0.6 add_convert_fusion.1
  370.9 1.3 collective-permute-done.17
  372.5 1.3 collective-permute-start.19
  373.8 1.7 collective-permute-start.22
  375.6 10.1 %collective-permute-done.15 = bf16[1024,512]{1,0:T(8,128)(2,1)S(1)} collective-permute-done((bf16[1024,512]{1,0:T(8,128)(2,1)S(1)}, bf16[1024,512]{1,0:T(8,128)(2,1)S(1)}, u32[]{:S(2)}, u32[]{:S(2)}) %collective-permute-start.15) | collective-permute-done | bytes 1048608 | tf_op jit(solution)/shard_map/ppermute | solution.py:360
  386.0 0.9 fusion.9
  386.8 2.4 collective-permute-start.20
  389.3 7.7 %collective-permute-done.19 = bf16[1024,512]{1,0:T(8,128)(2,1)S(1)} collective-permute-done((bf16[1024,512]{1,0:T(8,128)(2,1)S(1)}, bf16[1024,512]{1,0:T(8,128)(2,1)S(1)}, u32[]{:S(2)}, u32[]{:S(2)}) %collective-permute-start.19) | collective-permute-done | bytes 1048608 | tf_op jit(solution)/shard_map/ppermute | solution.py:360
  397.2 0.9 fusion.10
  398.1 2.4 collective-permute-start.21
  400.5 0.3 maximum_select_fusion.1
  400.9 8.6 %collective-permute-done.21 = bf16[512,512]{1,0:T(8,128)(2,1)} collective-permute-done((bf16[512,512]{1,0:T(8,128)(2,1)}, bf16[512,512]{1,0:T(8,128)(2,1)}, u32[]{:S(2)}, u32[]{:S(2)}) %collective-permute-start.21) | collective-permute-done | bytes 524320 | tf_op jit(solution)/shard_map/ppermute | solution.py:351
  409.5 1.6 maximum_select_fusion.2
  411.0 2.1 maximum_select_fusion
  (69 shorter events, 1.6 us)
Async XLA Ops:
  7.2 188.6 %all-gather.2.cloned.1.call-start = ((), (), s32[]{:S(2)}) async-start(), calls=%async_computation | async-start | bytes 6291456 | tf_op jit(solution)/shard_map/all_gather | solution.py:441
  10.3 158.3 %copy-start.4 = (bf16[4096,1,128]{2,0,1:T(8,128)(2,1)S(1)}, bf16[4096,1,128]{2,0,1:T(8,128)(2,1)}, u32[]{:S(2)}) copy-start(bf16[4096,1,128]{2,0,1:T(8,128)(2,1)} %param.12) | copy-start | bytes 3145732
  10.3 158.3 %copy-start.5 = (bf16[4096,1,128]{2,0,1:T(8,128)(2,1)S(1)}, bf16[4096,1,128]{2,0,1:T(8,128)(2,1)}, u32[]{:S(2)}) copy-start(bf16[4096,1,128]{2,0,1:T(8,128)(2,1)} %param.11) | copy-start | bytes 3145732
  10.3 185.4 %collective-permute-start.4 = (bf16[1024,1024]{1,0:T(8,128)(2,1)}, bf16[1024,1024]{1,0:T(8,128)(2,1)}, u32[]{:S(2)}, u32[]{:S(2)}) collective-permute-start(bf16[1024,1024]{1,0:T(8,128)(2,1)} %param.15), channel_id=1, source_target_pairs={{0,8},{4,12},{8,0},{12,4},{16,24},{20,28},{24,16},{28,20},{1,9},{5... | collective-permute-start | bytes 6291464 | tf_op jit(solution)/shard_map/ppermute | solution.py:431
  12.0 183.8 %collective-permute-start.5 = (bf16[1024,1024]{1,0:T(8,128)(2,1)}, bf16[1024,1024]{1,0:T(8,128)(2,1)}, u32[]{:S(2)}, u32[]{:S(2)}) collective-permute-start(bf16[1024,1024]{1,0:T(8,128)(2,1)} %param.15), channel_id=1, source_target_pairs={{0,24},{4,28},{8,16},{12,20},{16,8},{20,12},{24,0},{28,4},{1,25},{... | collective-permute-start | bytes 6291464 | tf_op jit(solution)/shard_map/ppermute | solution.py:431
  14.4 210.1 %collective-permute-start = (bf16[1024,1024]{1,0:T(8,128)(2,1)}, bf16[1024,1024]{1,0:T(8,128)(2,1)}, u32[]{:S(2)}, u32[]{:S(2)}) collective-permute-start(bf16[1024,1024]{1,0:T(8,128)(2,1)} %param.15), channel_id=1, source_target_pairs={{0,16},{4,20},{24,8},{28,12},{1,17},{5,21},{25,9},{29,13},{2,18},{... | collective-permute-start | bytes 6291464 | tf_op jit(solution)/shard_map/ppermute | solution.py:329
  20.4 136.3 %collective-permute-start.1 = (bf16[128,1024]{1,0:T(8,128)(2,1)}, bf16[128,1024]{1,0:T(8,128)(2,1)S(1)}, u32[]{:S(2)}, u32[]{:S(2)}) collective-permute-start(bf16[128,1024]{1,0:T(8,128)(2,1)} %get-tuple-element.34), channel_id=1, source_target_pairs={{0,24},{4,28},{8,16},{12,20},{16,8},{20,12},{24,0},{28,4},{1,25},{... | collective-permute-start | bytes 786440 | tf_op jit(solution)/shard_map/ppermute | solution.py:431
  23.4 152.9 %collective-permute-start.2 = (bf16[128,1024]{1,0:T(8,128)(2,1)}, bf16[128,1024]{1,0:T(8,128)(2,1)S(1)}, u32[]{:S(2)}, u32[]{:S(2)}) collective-permute-start(bf16[128,1024]{1,0:T(8,128)(2,1)} %get-tuple-element.35), channel_id=1, source_target_pairs={{0,16},{4,20},{8,24},{12,28},{16,0},{20,4},{24,8},{28,12},{1,17},{... | collective-permute-start | bytes 786440 | tf_op jit(solution)/shard_map/ppermute | solution.py:431
  156.7 21.1 %copy-start.12 = (bf16[128,1024]{1,0:T(8,128)(2,1)}, bf16[128,1024]{1,0:T(8,128)(2,1)S(1)}, u32[]{:S(2)}) copy-start(bf16[128,1024]{1,0:T(8,128)(2,1)S(1)} %collective-permute-done.1.refs_0_) | copy-start | bytes 786436
  156.7 21.1 %collective-permute-start.3 = (bf16[128,1024]{1,0:T(8,128)(2,1)}, bf16[128,1024]{1,0:T(8,128)(2,1)S(1)}, u32[]{:S(2)}, u32[]{:S(2)}) collective-permute-start(bf16[128,1024]{1,0:T(8,128)(2,1)} %get-tuple-element.36), channel_id=1, source_target_pairs={{0,8},{4,12},{8,0},{12,4},{16,24},{20,28},{24,16},{28,20},{1,9},{5... | collective-permute-start | bytes 786440 | tf_op jit(solution)/shard_map/ppermute | solution.py:431
  168.6 1.0 copy-start.6
  169.6 0.6 copy-start.10
  176.4 19.3 %copy-start.14 = (bf16[128,1024]{1,0:T(8,128)(2,1)}, bf16[128,1024]{1,0:T(8,128)(2,1)S(1)}, u32[]{:S(2)}) copy-start(bf16[128,1024]{1,0:T(8,128)(2,1)S(1)} %collective-permute-done.2.refs_1_) | copy-start | bytes 786436
  177.8 17.9 %copy-start.11 = (s32[20]{0:T(128)S(1)}, s32[20]{0:T(128)}, u32[]{:S(2)}) copy-start(s32[20]{0:T(128)} %get-tuple-element.30.meta_ref) | copy-start | bytes 244
  195.8 1.4 copy-start.1
  197.2 0.9 copy-start.13
  198.1 0.9 copy-start.15
  199.1 16.4 %copy-start.2 = (f32[3072,128]{1,0:T(8,128)S(1)}, f32[3072,128]{1,0:T(8,128)}, u32[]{:S(2)}) copy-start(f32[3072,128]{1,0:T(8,128)} %get-tuple-element.46.refs_3_.refs_4_) | copy-start | bytes 4718596
  199.1 16.4 %copy-start.3 = (f32[3072,128]{1,0:T(8,128)S(1)}, f32[3072,128]{1,0:T(8,128)}, u32[]{:S(2)}) copy-start(f32[3072,128]{1,0:T(8,128)} %get-tuple-element.47.refs_4_.refs_5_) | copy-start | bytes 4718596
  213.0 21.6 %collective-permute-start.7 = (bf16[144,1024]{1,0:T(8,128)(2,1)S(1)}, bf16[144,1024]{1,0:T(8,128)(2,1)S(1)}, u32[]{:S(2)}, u32[]{:S(2)}) collective-permute-start(bf16[144,1024]{1,0:T(8,128)(2,1)S(1)} %get-tuple-element.48), channel_id=1, source_target_pairs={{0,16},{4,20},{8,24},{12,28},{16,0},{20,4},{24,8},{28,12},{1,17},{... | collective-permute-start | bytes 884744 | tf_op jit(solution)/shard_map/ppermute | solution.py:431
  213.2 11.3 %copy-start.7 = (bf16[128,1024]{1,0:T(8,128)(2,1)S(1)}, bf16[128,1024]{1,0:T(8,128)(2,1)}, u32[]{:S(2)}) copy-start(bf16[128,1024]{1,0:T(8,128)(2,1)} %get-tuple-element.31.refs_0_) | copy-start | bytes 786436
  213.2 21.5 %collective-permute-start.8 = (bf16[144,1024]{1,0:T(8,128)(2,1)S(1)}, bf16[144,1024]{1,0:T(8,128)(2,1)S(1)}, u32[]{:S(2)}, u32[]{:S(2)}) collective-permute-start(bf16[144,1024]{1,0:T(8,128)(2,1)S(1)} %get-tuple-element.49), channel_id=1, source_target_pairs={{0,24},{4,28},{8,16},{12,20},{16,8},{20,12},{24,0},{28,4},{1,25},{... | collective-permute-start | bytes 884744 | tf_op jit(solution)/shard_map/ppermute | solution.py:431
  223.7 17.2 %collective-permute-start.6 = (bf16[144,1024]{1,0:T(8,128)(2,1)S(1)}, bf16[144,1024]{1,0:T(8,128)(2,1)S(1)}, u32[]{:S(2)}, u32[]{:S(2)}) collective-permute-start(bf16[144,1024]{1,0:T(8,128)(2,1)S(1)} %attend_last.4), channel_id=1, source_target_pairs={{0,8},{4,12},{8,0},{12,4},{16,24},{20,28},{24,16},{28,20},{1,9},{5... | collective-permute-start | bytes 884744 | tf_op jit(solution)/shard_map/ppermute | solution.py:431
  224.5 16.4 %copy-start = (bf16[8,64,1,1024]{3,1,2,0:T(8,128)(2,1)S(1)}, bf16[8,64,1,1024]{3,1,2,0:T(8,128)(2,1)}, u32[]{:S(2)}) copy-start(bf16[8,64,1,1024]{3,1,2,0:T(8,128)(2,1)} %param.8) | copy-start | bytes 3145732
  224.5 16.4 %copy-start.8 = (bf16[8,64,1,128]{3,1,2,0:T(8,128)(2,1)S(1)}, bf16[8,64,1,128]{3,1,2,0:T(8,128)(2,1)}, u32[]{:S(2)}) copy-start(bf16[8,64,1,128]{3,1,2,0:T(8,128)(2,1)} %param.9) | copy-start | bytes 393220
  224.5 16.4 %copy-start.9 = (bf16[8,64,1,128]{3,1,2,0:T(8,128)(2,1)S(1)}, bf16[8,64,1,128]{3,1,2,0:T(8,128)(2,1)}, u32[]{:S(2)}) copy-start(bf16[8,64,1,128]{3,1,2,0:T(8,128)(2,1)} %param.10) | copy-start | bytes 393220
  232.6 13.7 %copy-start.24 = (bf16[1024,1024]{1,0:T(8,128)(2,1)S(1)}, bf16[1024,1024]{1,0:T(8,128)(2,1)}, u32[]{:S(2)}) copy-start(bf16[1024,1024]{1,0:T(8,128)(2,1)} %param.15) | copy-start | bytes 6291460
  248.8 3.6 copy-start.22
  258.0 5.0 %collective-permute-start.11 = (bf16[512,2048]{1,0:T(8,128)(2,1)}, bf16[512,2048]{1,0:T(8,128)(2,1)S(1)}, u32[]{:S(2)}, u32[]{:S(2)}) collective-permute-start(bf16[512,2048]{1,0:T(8,128)(2,1)} %pad_maximum_fusion.1), channel_id=1, source_target_pairs={{1,0},{0,1},{3,2},{2,3},{5,4},{4,5},{7,6},{6,7},{9,8},{8,9},{11,10... | collective-permute-start | bytes 6291464 | tf_op jit(solution)/shard_map/ppermute | solution.py:360
  261.1 27.8 %collective-permute-start.10 = (bf16[1024,512]{1,0:T(8,128)(2,1)}, bf16[1024,512]{1,0:T(8,128)(2,1)}, u32[]{:S(2)}, u32[]{:S(2)}) collective-permute-start(bf16[1024,512]{1,0:T(8,128)(2,1)} %get-tuple-element.67), channel_id=1, source_target_pairs={{8,0},{12,4},{16,24},{20,28},{9,1},{13,5},{17,25},{21,29},{10,2},{... | collective-permute-start | bytes 3145736 | tf_op jit(solution)/shard_map/ppermute | solution.py:329
  262.4 26.5 %collective-permute-start.9 = (bf16[512,1024]{1,0:T(8,128)(2,1)}, bf16[512,1024]{1,0:T(8,128)(2,1)}, u32[]{:S(2)}, u32[]{:S(2)}) collective-permute-start(bf16[512,1024]{1,0:T(8,128)(2,1)} %bitcast.7), channel_id=1, source_target_pairs={{0,4},{4,0},{8,12},{12,8},{16,20},{20,16},{24,28},{28,24},{1,5},{5... | collective-permute-start | bytes 3145736 | tf_op jit(solution)/shard_map/ppermute | solution.py:470
  263.0 1.3 copy-start.18
  264.3 24.6 %copy-start.25 = (bf16[1024,1024]{1,0:T(8,128)(2,1)S(1)}, bf16[1024,1024]{1,0:T(8,128)(2,1)}, u32[]{:S(2)}) copy-start(bf16[1024,1024]{1,0:T(8,128)(2,1)} %param.15) | copy-start | bytes 6291460
  291.3 3.6 copy-start.19
  294.9 4.5 %copy-start.16 = (bf16[512,1024]{1,0:T(8,128)(2,1)}, bf16[512,1024]{1,0:T(8,128)(2,1)S(1)}, u32[]{:S(2)}) copy-start(bf16[512,1024]{1,0:T(8,128)(2,1)S(1)} %convolution_convert_fusion.2) | copy-start | bytes 3145732
  301.0 27.7 %collective-permute-start.12 = (bf16[512,2048]{1,0:T(8,128)(2,1)}, bf16[512,2048]{1,0:T(8,128)(2,1)}, u32[]{:S(2)}, u32[]{:S(2)}) collective-permute-start(bf16[512,2048]{1,0:T(8,128)(2,1)} %pad_maximum_fusion.3), channel_id=1, source_target_pairs={{1,0},{0,1},{3,2},{2,3},{5,4},{4,5},{7,6},{6,7},{9,8},{8,9},{11,10... | collective-permute-start | bytes 6291464 | tf_op jit(solution)/shard_map/ppermute | solution.py:360
  301.0 25.8 %collective-permute-start.13 = (bf16[512,1024]{1,0:T(8,128)(2,1)}, bf16[512,1024]{1,0:T(8,128)(2,1)}, u32[]{:S(2)}, u32[]{:S(2)}) collective-permute-start(bf16[512,1024]{1,0:T(8,128)(2,1)} %get-tuple-element.60), channel_id=1, source_target_pairs={{2,0},{3,1},{1,3},{6,4},{7,5},{5,7},{10,8},{11,9},{8,10},{14,12},{... | collective-permute-start | bytes 3145736 | tf_op jit(solution)/shard_map/ppermute | solution.py:360
  304.6 24.0 %copy-start.17 = (bf16[512,1024]{1,0:T(8,128)(2,1)S(1)}, bf16[512,1024]{1,0:T(8,128)(2,1)}, u32[]{:S(2)}) copy-start(bf16[512,1024]{1,0:T(8,128)(2,1)} %copy-done.16) | copy-start | bytes 3145732
  304.6 24.0 %copy-start.20 = (bf16[512,1024]{1,0:T(8,128)(2,1)S(1)}, bf16[512,1024]{1,0:T(8,128)(2,1)}, u32[]{:S(2)}) copy-start(bf16[512,1024]{1,0:T(8,128)(2,1)} %copy-done.19) | copy-start | bytes 3145732
  304.6 24.0 %copy-start.21 = (bf16[512,1024]{1,0:T(8,128)(2,1)S(1)}, bf16[512,1024]{1,0:T(8,128)(2,1)}, u32[]{:S(2)}) copy-start(bf16[512,1024]{1,0:T(8,128)(2,1)} %get-tuple-element.75) | copy-start | bytes 3145732
  331.6 4.8 %copy-start.23 = (bf16[1024,512]{1,0:T(8,128)(2,1)S(1)}, bf16[1024,512]{1,0:T(8,128)(2,1)}, u32[]{:S(2)}) copy-start(bf16[1024,512]{1,0:T(8,128)(2,1)} %get-tuple-element.66) | copy-start | bytes 3145732
  335.2 7.1 %collective-permute-start.14 = (bf16[1024,512]{1,0:T(8,128)(2,1)S(1)}, bf16[1024,512]{1,0:T(8,128)(2,1)S(1)}, u32[]{:S(2)}, u32[]{:S(2)}) collective-permute-start(bf16[1024,512]{1,0:T(8,128)(2,1)S(1)} %convolution_convert_fusion.1), channel_id=1, source_target_pairs={{1,0},{3,2},{5,4},{7,6},{8,9},{10,11},{12,13},{14,15},{17,16},{19,... | collective-permute-start | bytes 3145736 | tf_op jit(solution)/shard_map/ppermute | solution.py:360
  336.5 28.1 %collective-permute-start.16 = (bf16[1024,512]{1,0:T(8,128)(2,1)S(1)}, bf16[1024,512]{1,0:T(8,128)(2,1)S(1)}, u32[]{:S(2)}, u32[]{:S(2)}) collective-permute-start(bf16[1024,512]{1,0:T(8,128)(2,1)S(1)} %copy-done.23), channel_id=1, source_target_pairs={{8,0},{12,4},{16,24},{20,28},{9,1},{13,5},{17,25},{21,29},{10,2},{... | collective-permute-start | bytes 3145736 | tf_op jit(solution)/shard_map/ppermute | solution.py:329
  337.8 32.5 %collective-permute-start.18 = (bf16[512,1024]{1,0:T(8,128)(2,1)S(1)}, bf16[512,1024]{1,0:T(8,128)(2,1)S(1)}, u32[]{:S(2)}, u32[]{:S(2)}) collective-permute-start(bf16[512,1024]{1,0:T(8,128)(2,1)S(1)} %get-tuple-element.63), channel_id=1, source_target_pairs={{2,0},{3,1},{1,3},{6,4},{7,5},{5,7},{10,8},{11,9},{8,10},{14,12},{... | collective-permute-start | bytes 3145736 | tf_op jit(solution)/shard_map/ppermute | solution.py:360
  367.7 4.6 %collective-permute-start.17 = (bf16[1024,512]{1,0:T(8,128)(2,1)S(1)}, bf16[1024,512]{1,0:T(8,128)(2,1)S(1)}, u32[]{:S(2)}, u32[]{:S(2)}) collective-permute-start(bf16[1024,512]{1,0:T(8,128)(2,1)S(1)} %convolution_convert_fusion), channel_id=1, source_target_pairs={{1,0},{3,2},{5,4},{7,6},{8,9},{10,11},{12,13},{14,15},{17,16},{19,... | collective-permute-start | bytes 3145736 | tf_op jit(solution)/shard_map/ppermute | solution.py:360
  369.0 16.7 %collective-permute-start.15 = (bf16[1024,512]{1,0:T(8,128)(2,1)S(1)}, bf16[1024,512]{1,0:T(8,128)(2,1)S(1)}, u32[]{:S(2)}, u32[]{:S(2)}) collective-permute-start(bf16[1024,512]{1,0:T(8,128)(2,1)S(1)} %add_convert_fusion.4), channel_id=1, source_target_pairs={{0,2},{4,6},{9,11},{13,15},{18,16},{22,20},{27,25},{31,29}} | collective-permute-start | bytes 3145736 | tf_op jit(solution)/shard_map/ppermute | solution.py:360
  372.5 24.4 %collective-permute-start.19 = (bf16[1024,512]{1,0:T(8,128)(2,1)S(1)}, bf16[1024,512]{1,0:T(8,128)(2,1)S(1)}, u32[]{:S(2)}, u32[]{:S(2)}) collective-permute-start(bf16[1024,512]{1,0:T(8,128)(2,1)S(1)} %add_convert_fusion.2), channel_id=1, source_target_pairs={{0,2},{4,6},{9,11},{13,15},{18,16},{22,20},{27,25},{31,29}} | collective-permute-start | bytes 3145736 | tf_op jit(solution)/shard_map/ppermute | solution.py:360
  373.8 27.0 %collective-permute-start.22 = (bf16[512,1024]{1,0:T(8,128)(2,1)S(1)}, bf16[512,1024]{1,0:T(8,128)(2,1)}, u32[]{:S(2)}, u32[]{:S(2)}) collective-permute-start(bf16[512,1024]{1,0:T(8,128)(2,1)S(1)} %add_convert_fusion.1), channel_id=1, source_target_pairs={{0,4},{1,5},{3,7},{4,0},{5,1},{7,3},{8,12},{9,13},{10,14},{12,8},{... | collective-permute-start | bytes 3145736 | tf_op jit(solution)/shard_map/ppermute | solution.py:351
  386.8 14.0 %collective-permute-start.20 = (bf16[512,512]{1,0:T(8,128)(2,1)}, bf16[512,512]{1,0:T(8,128)(2,1)}, u32[]{:S(2)}, u32[]{:S(2)}) collective-permute-start(bf16[512,512]{1,0:T(8,128)(2,1)} %get-tuple-element.69), channel_id=1, source_target_pairs={{2,6},{6,2},{11,15},{15,11},{16,20},{20,16},{25,29},{29,25}} | collective-permute-start | bytes 1572872 | tf_op jit(solution)/shard_map/ppermute | solution.py:351
  398.1 11.4 %collective-permute-start.21 = (bf16[512,512]{1,0:T(8,128)(2,1)}, bf16[512,512]{1,0:T(8,128)(2,1)}, u32[]{:S(2)}, u32[]{:S(2)}) collective-permute-start(bf16[512,512]{1,0:T(8,128)(2,1)} %get-tuple-element.71), channel_id=1, source_target_pairs={{2,6},{6,2},{11,15},{15,11},{16,20},{20,16},{25,29},{29,25}} | collective-permute-start | bytes 1572872 | tf_op jit(solution)/shard_map/ppermute | solution.py:351
Sparse Core Ops, SparseCore 0:
  10.4 56.9 all-gather.1

commit v2 on v1

--- a/solution.py
+++ b/solution.py
@@ -321,90 +321,103 @@
     )(meta, q, keys, values, *parts)
 
 
-INWARD = ((0, 2), (3, 1))
-OUTWARD = ((1, 0), (2, 3))
-
-
-def plane_hop(x, pairs):
-    return lax.ppermute(x, "ctx", [(a * 2 + h, b * 2 + h) for a, b in pairs for h in range(2)])
-
-
-def project(rows, other, blocks, plane, holder):
+def multiply_kernel(kept_first_ref, *refs):
+    *row_refs, weight_ref, kept_ref, sent_ref, rows = refs
+    count = row_refs[0].shape[0]
+
+    @pl.when(pl.program_id(0) == 0)
+    def _():
+        for first, order in ((1, (0, 1, 2, 3)), (0, (2, 3, 0, 1))):
+
+            @pl.when(kept_first_ref[0] == first)
+            def _(order=order):
+                for place, i in enumerate(order):
+                    rows[place * count : (place + 1) * count, :] = row_refs[i][...]
+
+    for place, ref in ((1, sent_ref), (0, kept_ref)):
+        for part in range(2):
+            at = slice(part * count, (part + 1) * count)
+            x = rows[2 * place * count + part * count : 2 * place * count + (part + 1) * count, :]
+            ref[at, :] = jnp.dot(x, weight_ref[0], preferred_element_type=jnp.float32).astype(ref.dtype)
+
+
+def multiply(kept_first, row_parts, weights):
+    count, depth = row_parts[0].shape
+    blocks, _, width = weights.shape
+    rows = pl.BlockSpec((count, depth), lambda j: (0, 0))
+    out = pl.BlockSpec((2 * count, width), lambda j: (0, j))
+    return pl.pallas_call(
+        multiply_kernel,
+        grid=(blocks,),
+        out_shape=[jax.ShapeDtypeStruct((2 * count, blocks * width), jnp.bfloat16)] * 2,
+        in_specs=[pl.BlockSpec(memory_space=pltpu.SMEM)]
+        + [rows] * 4
+        + [pl.BlockSpec((1, depth, width), lambda j: (j, 0, 0))],
+        out_specs=[out] * 2,
+        scratch_shapes=[pltpu.VMEM((4 * count, depth), jnp.bfloat16)],
+        compiler_params=pltpu.CompilerParams(vmem_limit_bytes=32 * 1024 * 1024),
+        cost_estimate=pl.CostEstimate(
+            flops=8 * count * depth * blocks * width,
+            bytes_accessed=2 * blocks * depth * width,
+            transcendentals=0,
+        ),
+        name="multiply",
+    )(kept_first.reshape(1), *row_parts, weights)
+
+
+def project(rows, weights, plane, holder):
     group = lax.axis_index("kvh")
-    groups = lax.axis_size("kvh")
-    count = rows.shape[0]
-    apart = plane ^ group
-    even = apart & 1 == 0
-    low = apart < 2
-    block0, block1, block3, two_in, out_a, out_b = blocks
-    half = out_a.shape[1]
-    inner = (plane == 1) | (plane == 2)
-
-    def swap_holders(x, keep):
-        pairs = [
-            ((p * 2 + h) * groups + k, (p * 2 + 1 - h) * groups + k)
-            for p in range(groups)
-            for h in range(2)
-            for k in range(groups)
-            if keep(p ^ k)
-        ]
+    chip = group // 2
+    same = group % 2 == plane % 2
+    parts = 2
+    count = rows.shape[0] // parts
+    width = weights.shape[2]
+
+    def send(x, to, keep=lambda p, k: True):
+        pairs = []
+        for p in range(4):
+            for h in range(2):
+                for k in range(4):
+                    if keep(p, k):
+                        q, g, m = to(p, h, k)
+                        pairs.append(((p * 2 + h) * 4 + k, (q * 2 + g) * 4 + m))
         return lax.ppermute(x, ("ctx", "kvh"), pairs)
 
-    def to_group(x, flip, keep):
-        pairs = [
-            (c * groups + (k ^ flip), c * groups + k)
-            for c in range(2 * groups)
-            for k in range(groups)
-            if keep(c // 2 ^ k)
-        ]
-        return lax.ppermute(x, ("ctx", "kvh"), pairs)
-
-    def terms(x, block):
-        return jnp.dot(x, block, preferred_element_type=jnp.float32).astype(jnp.bfloat16)
+    def fetch(x):
+        return (
+            x,
+            send(x, lambda p, h, k: (p, 1 - h, k)),
+            send(x, lambda p, h, k: (p ^ 1, h, k)),
+            send(x, lambda p, h, k: (p ^ 1, 1 - h, k)),
+        )
 
     def add(a, b):
         return (a.astype(jnp.float32) + b.astype(jnp.float32)).astype(jnp.bfloat16)
 
-    def pair_sums(x):
-        term0, term1, term3 = terms(x, block0), terms(x, block1), terms(x, block3)
-        sent = jnp.concatenate([jnp.where(even, term1, term0), term3], axis=1)
-        got = to_group(sent, 1, lambda i: True)
-        width = term0.shape[1]
-        return add(jnp.where(even, term0, term1), got[:, :width]), add(term3, got[:, width:])
-
-    def chip_sums(near, far):
-        got = to_group(jnp.where(low, far, near), 2, lambda i: i != 2)
-        return add(jnp.where(low, near, far), got)
-
-    mine_sums = pair_sums(rows)
-    mine = chip_sums(*mine_sums)
-    other, out_a, *mine_sums = lax.optimization_barrier((other, out_a, *mine_sums))
-    their_sums = pair_sums(other)
-    theirs = chip_sums(*their_sums)
-    both = jnp.concatenate([rows, other], axis=0)
-
-    def last_block(came_in, came_out, *ready):
-        came_out = after(came_out, *ready)
-        term = terms(both, jnp.where(inner, came_in, came_out))
-        return add(term, to_group(term, 1, lambda i: i & 1 == 0))
-
-    def last_sums(total):
-        total = add(total, to_group(total, 2, lambda i: i == 2))
-        return total[:count], swap_holders(total[count:], lambda i: i == 2)
-
-    half_a = last_block(two_in[:, :half], out_a, *their_sums, mine)
-    half_b = last_block(two_in[:, half:], out_b, half_a)
-    half_b = after(half_b, theirs)
-    back = swap_holders(theirs, lambda i: i != 2)
-    mine_a, back_a = last_sums(half_a)
-    mine_b, back_b = last_sums(half_b)
-    mine = jnp.where(apart == 2, jnp.concatenate([mine_a, mine_b], axis=1), mine)
-    back = jnp.where(apart == 2, jnp.concatenate([back_a, back_b], axis=1), back)
-    return jnp.where(
-        holder == 0,
-        jnp.concatenate([mine, back], axis=1),
-        jnp.concatenate([back, mine], axis=1),
-    )
+    def results(fetched):
+        kept, sent = multiply(same.astype(jnp.int32), fetched, weights)
+        total = add(kept, send(sent, lambda p, h, k: (p, h, k ^ 1)))
+        low, high = total[:, :width], total[:, width:]
+        away = send(jnp.where(chip == 0, high, low), lambda p, h, k: (p, h, k ^ 2))
+        return add(jnp.where(chip == 0, low, high), away)
+
+    def deliver(total):
+        direct = send(
+            total[:count], lambda p, h, k: (p ^ 1, h, k ^ 1), lambda p, k: k % 2 != p % 2
+        )
+        back = send(
+            total[count:],
+            lambda p, h, k: (p, 1 - h, k) if k % 2 == p % 2 else (p ^ 1, 1 - h, k ^ 1),
+        )
+        mine = jnp.where(same, total[:count], direct)
+        return jnp.where(
+            holder == 0,
+            jnp.concatenate([mine, back], axis=1),
+            jnp.concatenate([back, mine], axis=1),
+        )
+
+    fetched = [fetch(rows[i * count : (i + 1) * count]) for i in range(parts)]
+    return jnp.concatenate([deliver(results(x)) for x in fetched], axis=0)
 
 
 def local(
@@ -430,25 +443,33 @@
         pairs = [(p * holders + h, (p ^ i) * holders + h) for p in range(prompts) for h in range(holders)]
         return lax.ppermute(x, "ctx", pairs)
 
-    if by_plane:
-        one, three = cross(out_weight, 1), cross(out_weight, 3)
-        two_in = plane_hop(out_weight, INWARD)
     chunks, meta = pack(prompt_of, prefix_len, own_queries, capacity, holders, slot_count)
     chunks = chunks[:1] + [cross(x, i) for i, x in enumerate(chunks) if i > 0]
     near = prefix_keys[:, 0], prefix_values[:, 0]
-    lines = [[p * holders + h for h in range(holders)] for p in range(prompts)]
-    joined = jnp.concatenate(near, axis=1)
-    joined = lax.all_gather(joined, "ctx", axis=0, tiled=True, axis_index_groups=lines)
-    far = joined, joined
     away = chunks[:0:-1]
+    if by_plane:
+        pairs = [[p * holders + h, (p + 2) * holders + h] for p in range(2) for h in range(holders)]
+        weights = lax.all_gather(
+            after(out_weight, *away), "ctx", axis=0, tiled=False, axis_index_groups=pairs
+        )
+        shards = [near, [after(x, away[-1]) for x in near]]
+        shards[1] = [
+            lax.ppermute(x, "ctx", [(c, c ^ 1) for c in range(ctx_count)]) for x in shards[1]
+        ]
+    else:
+        lines = [[p * holders + h for h in range(holders)] for p in range(prompts)]
+        joined = jnp.concatenate(near, axis=1)
+        joined = lax.all_gather(joined, "ctx", axis=0, tiled=True, axis_index_groups=lines)
+        shards = [near] + [(joined, joined)] * (holders - 1)
 
     state_home = state_away = None
     for shard in range(holders - 1):
-        kv = near if shard == 0 else far
+        kv = shards[shard]
         state_home = attend(meta, places, chunks[:1], *kv, slot_count, shard, state_home, 0, False)
         state_home, away = lax.optimization_barrier((state_home, away))
         state_away = attend(meta, places, away, *kv, slot_count, shard, state_away, 0, False)
     shard = holders - 1
+    far = shards[shard]
     done = [None] * prompts
     for where, members in enumerate([range(prompts - 1, 1, -1), [1]]):
         queries_now = [away[prompts - 1 - i] for i in members]
@@ -456,22 +477,12 @@
         results = attend(meta, places, queries_now, *far, slot_count, shard, state_away, block, True)
         for i, x in zip(members, results):
             done[i] = cross(x, i)
-        if by_plane and where == 0:
-            one, three, state_away = lax.optimization_barrier((one, three, state_away))
-            half = out_weight.shape[1] // 2
-            two_out = [plane_hop(x, OUTWARD) for x in (three[:, :half], three[:, half:])]
-    if by_plane:
-        two_in, state_home = lax.optimization_barrier((two_in, state_home))
     (done[0],) = attend(meta, places, chunks[:1], *far, slot_count, shard, state_home, 0, True)
     attended = combine(meta, capacity, own_queries, own_keys, own_values, done)
     rows = attended.reshape(resp_count * tokens_each, width)
 
     if by_plane:
-        other = lax.ppermute(
-            rows, "ctx", [(p * 2 + h, p * 2 + 1 - h) for p in range(prompts) for h in range(2)]
-        )
-        blocks = out_weight, one, three, two_in, *two_out
-        projected = project(rows, other, blocks, my_prompt, my_holder)
+        projected = project(rows, weights, my_prompt, my_holder)
     else:
         weights = lax.all_gather(out_weight, "ctx", axis=1, tiled=True)
         terms = jnp.dot(rows, weights, preferred_element_type=jnp.float32)

time: 427 us -> 315 us (0.74)
  the two profiles are of different devices: /device:TPU:6 before, /device:TPU:0 now
where the time goes in v2:
time: 315 us; the launch traced here: 309 us
  waiting for transfers between devices  178 us (57%)
  Pallas kernels  73.1 us (23%)
  starting transfers between devices  24 us (8%)
  between operations  14.7 us (5%)
  local copies, waits for them, and re-layouts  10.5 us (3%)
  other arithmetic  8.71 us (3%)
    ppermute x14, waiting for transfers between devices, send(): return lax.ppermute(x, ('ctx', 'kvh'), pairs)  114 us
    pallas_call x5, Pallas kernels, attend(): pl.pallas_call(functools.partial(attend_kernel, count, first, last, shard...  51.8 us
    ppermute x6, waiting for transfers between devices, cross(): return lax.ppermute(x, 'ctx', pairs)  43.6 us
    ppermute x2, waiting for transfers between devices, local(): lax.ppermute(x, 'ctx', [(c, c ^ 1) for c in range(ctx_count)])  20.2 us
    pallas_call x2, Pallas kernels, multiply(): pl.pallas_call(multiply_kernel, grid=(blocks,), out_shape=[jax.ShapeDtype...  13.2 us
    ppermute x14, starting transfers between devices, send(): return lax.ppermute(x, ('ctx', 'kvh'), pairs)  12.6 us
    ppermute x6, starting transfers between devices, cross(): return lax.ppermute(x, 'ctx', pairs)  9.28 us
    unnamed x34, local copies, waits for them, and re-layouts  9.11 us
  transfers between devices with their start and end apart: 23, of which 14 were waited for; matrix products, arithmetic and copies ran while one was open for 3% of the time, Pallas kernels for 23%

profile of v2, /device:TPU:0, one launch (start us, length us, event | category | flops | bytes accessed | tf_op | source)
XLA Modules:
  0.0 308.9 jit_solution(17593984828007000623)
XLA Ops:
  7.2 2.6 pack.1
  9.9 3.1 %collective-permute-start = (bf16[128,1024]{1,0:T(8,128)(2,1)}, bf16[128,1024]{1,0:T(8,128)(2,1)S(1)}, u32[]{:S(2)}, u32[]{:S(2)}) collective-permute-start(bf16[128,1024]{1,0:T(8,128)(2,1)} %get-tuple-element.27), channel_id=1, source_target_pairs={{0,8},{4,12},{8,0},{12,4},{16,24},{20,28},{24,16},{28,20},{1,9},{5... | collective-permute-start | bytes 786440 | tf_op jit(solution)/shard_map/ppermute | solution.py:444
  13.0 2.5 collective-permute-start.3
  15.4 0.1 collective-permute-start.4
  15.6 4.4 %collective-permute-done.refs_2_.refs_0_ = bf16[128,1024]{1,0:T(8,128)(2,1)S(1)} collective-permute-done((bf16[128,1024]{1,0:T(8,128)(2,1)}, bf16[128,1024]{1,0:T(8,128)(2,1)S(1)}, u32[]{:S(2)}, u32[]{:S(2)}) %collective-permute-start) | collective-permute-done | bytes 262176 | tf_op jit(solution)/shard_map/ppermute | solution.py:444
  20.0 8.5 %collective-permute-done.3.refs_0_ = bf16[128,1024]{1,0:T(8,128)(2,1)S(1)} collective-permute-done((bf16[128,1024]{1,0:T(8,128)(2,1)}, bf16[128,1024]{1,0:T(8,128)(2,1)S(1)}, u32[]{:S(2)}, u32[]{:S(2)}) %collective-permute-start.3) | collective-permute-done | bytes 262176 | tf_op jit(solution)/shard_map/ppermute | solution.py:444
  28.5 10.1 %collective-permute-done.4.refs_1_ = bf16[128,1024]{1,0:T(8,128)(2,1)S(1)} collective-permute-done((bf16[128,1024]{1,0:T(8,128)(2,1)}, bf16[128,1024]{1,0:T(8,128)(2,1)S(1)}, u32[]{:S(2)}, u32[]{:S(2)}) %collective-permute-start.4) | collective-permute-done | bytes 262176 | tf_op jit(solution)/shard_map/ppermute | solution.py:444
  38.7 1.6 collective-permute-start.1
  40.3 0.5 collective-permute-start.2
  40.8 6.2 %attend.2 = (f32[1024,128]{1,0:T(8,128)S(1)}, f32[1024,128]{1,0:T(8,128)S(1)}) custom-call(s32[20]{0:T(128)S(1)} %copy-done.5, bf16[128,1024]{1,0:T(8,128)(2,1)S(1)} %copy-done.16, bf16[4096,128]{1,0:T(8,128)(2,1)S(1)} %bitcast.27, bf16[4096,128]{1,0:T(8,128)(2,1)S(1)} %bitcast.30), custom_call_target="tpu_custom_call" | custom-call | flops 2147483648 | bytes 2097152 | tf_op jit(solution)/shard_map/attend/pallas_call | solution.py:238
  46.9 18.1 %attend.3 = (f32[3072,128]{1,0:T(8,128)}, f32[3072,128]{1,0:T(8,128)}) custom-call(s32[20]{0:T(128)S(1)} %copy-done.5, bf16[128,1024]{1,0:T(8,128)(2,1)S(1)} %collective-permute-done.3.refs_0_, bf16[128,1024]{1,0:T(8,128)(2,1)S(1)} %collective-permute-done.4.refs_1_, bf16[128,1024]{1,0:T(8,128)(2,1)S(1)} %collective-permute-done.refs_2_.refs_0_, ...), custom_call_target="tpu_custom_call" | custom-call | flops 6442450944 | bytes 2097152 | tf_op jit(solution)/shard_map/attend/pallas_call | solution.py:238
  65.1 20.2 %collective-permute-done.2.refs_2_.refs_3_ = bf16[4096,128]{1,0:T(8,128)(2,1)S(1)} collective-permute-done((bf16[4096,128]{1,0:T(8,128)(2,1)S(1)}, bf16[4096,128]{1,0:T(8,128)(2,1)S(1)}, u32[]{:S(2)}, u32[]{:S(2)}) %collective-permute-start.2) | collective-permute-done | bytes 1048608 | tf_op jit(solution)/shard_map/ppermute | solution.py:457
  85.2 13.1 %attend_last.5 = (bf16[144,1024]{1,0:T(8,128)(2,1)S(1)}, bf16[144,1024]{1,0:T(8,128)(2,1)S(1)}) custom-call(s32[20]{0:T(128)S(1)} %copy-done.5, bf16[128,1024]{1,0:T(8,128)(2,1)S(1)} %collective-permute-done.3.refs_0_, bf16[128,1024]{1,0:T(8,128)(2,1)S(1)} %collective-permute-done.4.refs_1_, bf16[4096,128]{1,0:T(8,128)(2,1)S(1)} %collective-permute-done.1.refs_1_.refs_2_, ...), custom_call_target="tpu_custom_call" | custom-call | flops 4294967296 | bytes 2097152 | tf_op jit(solution)/shard_map/attend_last/pallas_call | solution.py:238
  98.3 0.1 collective-permute-start.6
  98.4 2.0 collective-permute-start.7
  100.5 7.9 %attend_last.4 = bf16[144,1024]{1,0:T(8,128)(2,1)S(1)} custom-call(s32[20]{0:T(128)S(1)} %copy-done.5, bf16[128,1024]{1,0:T(8,128)(2,1)S(1)} %collective-permute-done.refs_2_.refs_0_, bf16[4096,128]{1,0:T(8,128)(2,1)S(1)} %collective-permute-done.1.refs_1_.refs_2_, bf16[4096,128]{1,0:T(8,128)(2,1)S(1)} %collective-permute-done.2.refs_2_.refs_3_, ...), custom_call_target="tpu_custom_call" | custom-call | flops 2147483648 | bytes 2097152 | tf_op jit(solution)/shard_map/attend_last/pallas_call | solution.py:238
  108.4 1.5 collective-permute-start.5
  109.9 6.5 %attend_last.3.refs_0_ = bf16[144,1024]{1,0:T(8,128)(2,1)S(1)} custom-call(s32[20]{0:T(128)S(1)} %copy-done.5, bf16[128,1024]{1,0:T(8,128)(2,1)S(1)} %copy-done.16, bf16[4096,128]{1,0:T(8,128)(2,1)S(1)} %collective-permute-done.1.refs_1_.refs_2_, bf16[4096,128]{1,0:T(8,128)(2,1)S(1)} %collective-permute-done.2.refs_2_.refs_3_, ...), custom_call_target="tpu_custom_call" | custom-call | flops 2147483648 | bytes 2097152 | tf_op jit(solution)/shard_map/attend_last/pallas_call | solution.py:238
  116.4 8.1 %collective-permute-done.6.refs_2_ = bf16[144,1024]{1,0:T(8,128)(2,1)S(1)} collective-permute-done((bf16[144,1024]{1,0:T(8,128)(2,1)S(1)}, bf16[144,1024]{1,0:T(8,128)(2,1)S(1)}, u32[]{:S(2)}, u32[]{:S(2)}) %collective-permute-start.6) | collective-permute-done | bytes 294944 | tf_op jit(solution)/shard_map/ppermute | solution.py:444
  124.5 12.5 %collective-permute-done.5.refs_1_ = bf16[144,1024]{1,0:T(8,128)(2,1)S(1)} collective-permute-done((bf16[144,1024]{1,0:T(8,128)(2,1)S(1)}, bf16[144,1024]{1,0:T(8,128)(2,1)S(1)}, u32[]{:S(2)}, u32[]{:S(2)}) %collective-permute-start.5) | collective-permute-done | bytes 294944 | tf_op jit(solution)/shard_map/ppermute | solution.py:444
  137.0 5.4 %combine.1 = bf16[8,64,1024]{2,1,0:T(8,128)(2,1)} custom-call(s32[20]{0:T(128)S(1)} %copy-done.5, bf16[8,64,1024]{2,1,0:T(8,128)(2,1)S(1)} %bitcast.13, bf16[8,64,128]{2,1,0:T(8,128)(2,1)S(1)} %bitcast.22, bf16[8,64,128]{2,1,0:T(8,128)(2,1)S(1)} %bitcast.23, bf16[144,1024]{1,0:T(8,128)(2,1)S(1)} %attend_last.3.refs_0_, ...), custom_call_target="tpu_custom_call" | custom-call | flops 134217728 | bytes 4194304 | tf_op jit(solution)/shard_map/combine/pallas_call | solution.py:307
  142.5 1.3 fusion
  143.8 1.7 collective-permute-start.10
  145.4 0.5 collective-permute-start.8
  145.9 1.4 collective-permute-start.9
  147.3 1.5 collective-permute-start.15
  148.8 0.7 collective-permute-start.16
  149.5 29.5 %collective-permute-done.10.refs_3_ = bf16[256,1024]{1,0:T(8,128)(2,1)S(1)} collective-permute-done((bf16[256,1024]{1,0:T(8,128)(2,1)S(1)}, bf16[256,1024]{1,0:T(8,128)(2,1)S(1)}, u32[]{:S(2)}, u32[]{:S(2)}) %collective-permute-start.10) | collective-permute-done | bytes 524320 | tf_op jit(solution)/shard_map/ppermute | solution.py:384
  179.1 0.8 copy-done.10
  179.9 0.8 copy-done.12
  180.7 8.7 %collective-permute-done.9.refs_2_ = bf16[256,1024]{1,0:T(8,128)(2,1)S(1)} collective-permute-done((bf16[256,1024]{1,0:T(8,128)(2,1)S(1)}, bf16[256,1024]{1,0:T(8,128)(2,1)S(1)}, u32[]{:S(2)}, u32[]{:S(2)}) %collective-permute-start.9) | collective-permute-done | bytes 524320 | tf_op jit(solution)/shard_map/ppermute | solution.py:384
  189.3 0.8 copy-done.14
  190.2 2.2 copy-done.6
  192.3 1.0 copy-done.11
  193.4 1.0 copy-done.13
  194.4 1.0 copy-done.15
  195.5 5.9 %multiply.2 = (bf16[512,2048]{1,0:T(8,128)(2,1)S(1)}, bf16[512,2048]{1,0:T(8,128)(2,1)}) custom-call(s32[1]{0:T(128)} %bitcast.7.kept_first_ref, bf16[256,1024]{1,0:T(8,128)(2,1)S(1)} %bitcast.21, bf16[256,1024]{1,0:T(8,128)(2,1)S(1)} %copy-done.13, bf16[256,1024]{1,0:T(8,128)(2,1)S(1)} %copy-done.15, bf16[256,1024]{1,0:T(8,128)(2,1)S(1)} %copy-done.11, ...), custom_call_target="tpu_custom_call" | custom-call | flops 4294967296 | bytes 4194304 | tf_op jit(solution)/shard_map/multiply/pallas_call | solution.py:349
  201.4 0.1 collective-permute-start.11
  201.5 11.3 %collective-permute-done.17.refs_3_ = bf16[256,1024]{1,0:T(8,128)(2,1)} collective-permute-done((bf16[256,1024]{1,0:T(8,128)(2,1)S(1)}, bf16[256,1024]{1,0:T(8,128)(2,1)}, u32[]{:S(2)}, u32[]{:S(2)}) %collective-permute-start.17) | collective-permute-done | bytes 524320 | tf_op jit(solution)/shard_map/ppermute | solution.py:384
  212.8 7.3 %multiply.3 = (bf16[512,2048]{1,0:T(8,128)(2,1)S(1)}, bf16[512,2048]{1,0:T(8,128)(2,1)}) custom-call(s32[1]{0:T(128)} %bitcast.7.kept_first_ref, bf16[256,1024]{1,0:T(8,128)(2,1)S(1)} %bitcast.17, bf16[256,1024]{1,0:T(8,128)(2,1)} %collective-permute-done.15.refs_1_, bf16[256,1024]{1,0:T(8,128)(2,1)} %collective-permute-done.16.refs_2_, ...), custom_call_target="tpu_custom_call" | custom-call | flops 4294967296 | bytes 4194304 | tf_op jit(solution)/shard_map/multiply/pallas_call | solution.py:349
  220.1 1.3 copy-done.1
  221.4 0.1 collective-permute-start.18
  221.5 2.4 add_convert_fusion.1
  223.9 0.1 broadcast_select_fusion.1
  224.0 1.5 collective-permute-start.12
  225.6 0.3 collective-permute-done.18
  225.9 2.4 add_convert_fusion
  228.3 0.1 broadcast_select_fusion
  228.4 1.5 collective-permute-start.19
  229.9 20.1 %collective-permute-done.12 = bf16[512,1024]{1,0:T(8,128)(2,1)S(1)} collective-permute-done((bf16[512,1024]{1,0:T(8,128)(2,1)S(1)}, bf16[512,1024]{1,0:T(8,128)(2,1)S(1)}, u32[]{:S(2)}, u32[]{:S(2)}) %collective-permute-start.12) | collective-permute-done | bytes 1048608 | tf_op jit(solution)/shard_map/ppermute | solution.py:384
  250.0 0.6 add_convert_fusion.3
  250.7 0.7 collective-permute-start.13
  251.4 20.6 %collective-permute-done.19 = bf16[512,1024]{1,0:T(8,128)(2,1)S(1)} collective-permute-done((bf16[512,1024]{1,0:T(8,128)(2,1)S(1)}, bf16[512,1024]{1,0:T(8,128)(2,1)S(1)}, u32[]{:S(2)}, u32[]{:S(2)}) %collective-permute-start.19) | collective-permute-done | bytes 1048608 | tf_op jit(solution)/shard_map/ppermute | solution.py:384
  272.0 0.6 add_convert_fusion.2
  272.7 0.7 collective-permute-start.20
  273.4 0.1 broadcast_select_fusion.3
  273.5 0.6 collective-permute-start.14
  274.1 0.1 broadcast_select_fusion.2
  274.2 1.5 collective-permute-start.21
  275.8 7.0 %collective-permute-done.14 = bf16[256,1024]{1,0:T(8,128)(2,1)S(1)} collective-permute-done((bf16[256,1024]{1,0:T(8,128)(2,1)S(1)}, bf16[256,1024]{1,0:T(8,128)(2,1)S(1)}, u32[]{:S(2)}, u32[]{:S(2)}) %collective-permute-start.14) | collective-permute-done | bytes 524320 | tf_op jit(solution)/shard_map/ppermute | solution.py:384
  282.8 0.4 maximum_select_fusion
  283.2 16.5 %collective-permute-done.21 = bf16[256,1024]{1,0:T(8,128)(2,1)S(1)} collective-permute-done((bf16[256,1024]{1,0:T(8,128)(2,1)S(1)}, bf16[256,1024]{1,0:T(8,128)(2,1)S(1)}, u32[]{:S(2)}, u32[]{:S(2)}) %collective-permute-start.21) | collective-permute-done | bytes 524320 | tf_op jit(solution)/shard_map/ppermute | solution.py:384
  299.6 0.4 maximum_select_fusion.1
  300.0 1.6 pad_maximum_fusion
  (40 shorter events, 0.2 us)
Async XLA Ops:
  7.2 31.5 %copy-start.8 = (bf16[4096,1,128]{2,0,1:T(8,128)(2,1)S(1)}, bf16[4096,1,128]{2,0,1:T(8,128)(2,1)}, u32[]{:S(2)}) copy-start(bf16[4096,1,128]{2,0,1:T(8,128)(2,1)} %param.11) | copy-start | bytes 3145732
  7.2 33.1 %copy-start.9 = (bf16[4096,1,128]{2,0,1:T(8,128)(2,1)S(1)}, bf16[4096,1,128]{2,0,1:T(8,128)(2,1)}, u32[]{:S(2)}) copy-start(bf16[4096,1,128]{2,0,1:T(8,128)(2,1)} %param.12) | copy-start | bytes 3145732
  7.2 183.0 %all-gather.3.cloned.1.call-start = ((), (), s32[]{:S(2)}) async-start(), calls=%async_computation | async-start | bytes 6291456 | tf_op jit(solution)/shard_map/all_gather | solution.py:452
  9.8 30.9 %copy-start.5 = (s32[20]{0:T(128)S(1)}, s32[20]{0:T(128)}, u32[]{:S(2)}) copy-start(s32[20]{0:T(128)} %get-tuple-element.25.meta_ref) | copy-start | bytes 244
  9.9 30.9 %copy-start.16 = (bf16[128,1024]{1,0:T(8,128)(2,1)S(1)}, bf16[128,1024]{1,0:T(8,128)(2,1)}, u32[]{:S(2)}) copy-start(bf16[128,1024]{1,0:T(8,128)(2,1)} %get-tuple-element.26.refs_0_) | copy-start | bytes 786436
  9.9 10.1 %collective-permute-start = (bf16[128,1024]{1,0:T(8,128)(2,1)}, bf16[128,1024]{1,0:T(8,128)(2,1)S(1)}, u32[]{:S(2)}, u32[]{:S(2)}) collective-permute-start(bf16[128,1024]{1,0:T(8,128)(2,1)} %get-tuple-element.27), channel_id=1, source_target_pairs={{0,8},{4,12},{8,0},{12,4},{16,24},{20,28},{24,16},{28,20},{1,9},{5... | collective-permute-start | bytes 786440 | tf_op jit(solution)/shard_map/ppermute | solution.py:444
  13.0 15.6 %collective-permute-start.3 = (bf16[128,1024]{1,0:T(8,128)(2,1)}, bf16[128,1024]{1,0:T(8,128)(2,1)S(1)}, u32[]{:S(2)}, u32[]{:S(2)}) collective-permute-start(bf16[128,1024]{1,0:T(8,128)(2,1)} %get-tuple-element.32), channel_id=1, source_target_pairs={{0,24},{4,28},{8,16},{12,20},{16,8},{20,12},{24,0},{28,4},{1,25},{... | collective-permute-start | bytes 786440 | tf_op jit(solution)/shard_map/ppermute | solution.py:444
  15.4 23.2 %collective-permute-start.4 = (bf16[128,1024]{1,0:T(8,128)(2,1)}, bf16[128,1024]{1,0:T(8,128)(2,1)S(1)}, u32[]{:S(2)}, u32[]{:S(2)}) collective-permute-start(bf16[128,1024]{1,0:T(8,128)(2,1)} %get-tuple-element.33), channel_id=1, source_target_pairs={{0,16},{4,20},{8,24},{12,28},{16,0},{20,4},{24,8},{28,12},{1,17},{... | collective-permute-start | bytes 786440 | tf_op jit(solution)/shard_map/ppermute | solution.py:444
  38.7 26.4 %collective-permute-start.1 = (bf16[4096,128]{1,0:T(8,128)(2,1)S(1)}, bf16[4096,128]{1,0:T(8,128)(2,1)S(1)}, u32[]{:S(2)}, u32[]{:S(2)}) collective-permute-start(bf16[4096,128]{1,0:T(8,128)(2,1)S(1)} %bitcast.26), channel_id=1, source_target_pairs={{0,4},{4,0},{8,12},{12,8},{16,20},{20,16},{24,28},{28,24},{1,5},{5... | collective-permute-start | bytes 3145736 | tf_op jit(solution)/shard_map/ppermute | solution.py:457
  40.3 45.0 %collective-permute-start.2 = (bf16[4096,128]{1,0:T(8,128)(2,1)S(1)}, bf16[4096,128]{1,0:T(8,128)(2,1)S(1)}, u32[]{:S(2)}, u32[]{:S(2)}) collective-permute-start(bf16[4096,128]{1,0:T(8,128)(2,1)S(1)} %bitcast.29), channel_id=1, source_target_pairs={{0,4},{4,0},{8,12},{12,8},{16,20},{20,16},{24,28},{28,24},{1,5},{5... | collective-permute-start | bytes 3145736 | tf_op jit(solution)/shard_map/ppermute | solution.py:457
  98.3 26.2 %collective-permute-start.6 = (bf16[144,1024]{1,0:T(8,128)(2,1)S(1)}, bf16[144,1024]{1,0:T(8,128)(2,1)S(1)}, u32[]{:S(2)}, u32[]{:S(2)}) collective-permute-start(bf16[144,1024]{1,0:T(8,128)(2,1)S(1)} %get-tuple-element.41), channel_id=1, source_target_pairs={{0,16},{4,20},{8,24},{12,28},{16,0},{20,4},{24,8},{28,12},{1,17},{... | collective-permute-start | bytes 884744 | tf_op jit(solution)/shard_map/ppermute | solution.py:444
  98.4 26.1 %collective-permute-start.7 = (bf16[144,1024]{1,0:T(8,128)(2,1)S(1)}, bf16[144,1024]{1,0:T(8,128)(2,1)S(1)}, u32[]{:S(2)}, u32[]{:S(2)}) collective-permute-start(bf16[144,1024]{1,0:T(8,128)(2,1)S(1)} %get-tuple-element.42), channel_id=1, source_target_pairs={{0,24},{4,28},{8,16},{12,20},{16,8},{20,12},{24,0},{28,4},{1,25},{... | collective-permute-start | bytes 884744 | tf_op jit(solution)/shard_map/ppermute | solution.py:444
  108.4 28.6 %copy-start = (bf16[8,64,1,1024]{3,1,2,0:T(8,128)(2,1)S(1)}, bf16[8,64,1,1024]{3,1,2,0:T(8,128)(2,1)}, u32[]{:S(2)}) copy-start(bf16[8,64,1,1024]{3,1,2,0:T(8,128)(2,1)} %param.8) | copy-start | bytes 3145732
  108.4 28.6 %copy-start.3 = (bf16[8,64,1,128]{3,1,2,0:T(8,128)(2,1)S(1)}, bf16[8,64,1,128]{3,1,2,0:T(8,128)(2,1)}, u32[]{:S(2)}) copy-start(bf16[8,64,1,128]{3,1,2,0:T(8,128)(2,1)} %param.9) | copy-start | bytes 393220
  108.4 28.6 %copy-start.4 = (bf16[8,64,1,128]{3,1,2,0:T(8,128)(2,1)S(1)}, bf16[8,64,1,128]{3,1,2,0:T(8,128)(2,1)}, u32[]{:S(2)}) copy-start(bf16[8,64,1,128]{3,1,2,0:T(8,128)(2,1)} %param.10) | copy-start | bytes 393220
  108.4 28.6 %collective-permute-start.5 = (bf16[144,1024]{1,0:T(8,128)(2,1)S(1)}, bf16[144,1024]{1,0:T(8,128)(2,1)S(1)}, u32[]{:S(2)}, u32[]{:S(2)}) collective-permute-start(bf16[144,1024]{1,0:T(8,128)(2,1)S(1)} %attend_last.4), channel_id=1, source_target_pairs={{0,8},{4,12},{8,0},{12,4},{16,24},{20,28},{24,16},{28,20},{1,9},{5... | collective-permute-start | bytes 884744 | tf_op jit(solution)/shard_map/ppermute | solution.py:444
  143.8 35.3 %collective-permute-start.10 = (bf16[256,1024]{1,0:T(8,128)(2,1)S(1)}, bf16[256,1024]{1,0:T(8,128)(2,1)S(1)}, u32[]{:S(2)}, u32[]{:S(2)}) collective-permute-start(bf16[256,1024]{1,0:T(8,128)(2,1)S(1)} %bitcast.18), channel_id=1, source_target_pairs={{0,12},{1,13},{2,14},{3,15},{4,8},{5,9},{6,10},{7,11},{8,4},{9,5},... | collective-permute-start | bytes 1572872 | tf_op jit(solution)/shard_map/ppermute | solution.py:384
  145.4 34.4 %collective-permute-start.8 = (bf16[256,1024]{1,0:T(8,128)(2,1)S(1)}, bf16[256,1024]{1,0:T(8,128)(2,1)S(1)}, u32[]{:S(2)}, u32[]{:S(2)}) collective-permute-start(bf16[256,1024]{1,0:T(8,128)(2,1)S(1)} %bitcast.19), channel_id=1, source_target_pairs={{0,4},{1,5},{2,6},{3,7},{4,0},{5,1},{6,2},{7,3},{8,12},{9,13},{10,... | collective-permute-start | bytes 1572872 | tf_op jit(solution)/shard_map/ppermute | solution.py:384
  145.9 43.4 %collective-permute-start.9 = (bf16[256,1024]{1,0:T(8,128)(2,1)S(1)}, bf16[256,1024]{1,0:T(8,128)(2,1)S(1)}, u32[]{:S(2)}, u32[]{:S(2)}) collective-permute-start(bf16[256,1024]{1,0:T(8,128)(2,1)S(1)} %bitcast.20), channel_id=1, source_target_pairs={{0,8},{1,9},{2,10},{3,11},{4,12},{5,13},{6,14},{7,15},{8,0},{9,1},... | collective-permute-start | bytes 1572872 | tf_op jit(solution)/shard_map/ppermute | solution.py:384
  147.3 54.2 %collective-permute-start.15 = (bf16[256,1024]{1,0:T(8,128)(2,1)S(1)}, bf16[256,1024]{1,0:T(8,128)(2,1)}, u32[]{:S(2)}, u32[]{:S(2)}) collective-permute-start(bf16[256,1024]{1,0:T(8,128)(2,1)S(1)} %bitcast.14), channel_id=1, source_target_pairs={{0,4},{1,5},{2,6},{3,7},{4,0},{5,1},{6,2},{7,3},{8,12},{9,13},{10,... | collective-permute-start | bytes 1572872 | tf_op jit(solution)/shard_map/ppermute | solution.py:384
  148.8 52.7 %collective-permute-start.16 = (bf16[256,1024]{1,0:T(8,128)(2,1)S(1)}, bf16[256,1024]{1,0:T(8,128)(2,1)}, u32[]{:S(2)}, u32[]{:S(2)}) collective-permute-start(bf16[256,1024]{1,0:T(8,128)(2,1)S(1)} %bitcast.15), channel_id=1, source_target_pairs={{0,8},{1,9},{2,10},{3,11},{4,12},{5,13},{6,14},{7,15},{8,0},{9,1},... | collective-permute-start | bytes 1572872 | tf_op jit(solution)/shard_map/ppermute | solution.py:384
  179.0 0.8 copy-start.10
  179.9 32.9 %collective-permute-start.17 = (bf16[256,1024]{1,0:T(8,128)(2,1)S(1)}, bf16[256,1024]{1,0:T(8,128)(2,1)}, u32[]{:S(2)}, u32[]{:S(2)}) collective-permute-start(bf16[256,1024]{1,0:T(8,128)(2,1)S(1)} %bitcast.16), channel_id=1, source_target_pairs={{0,12},{1,13},{2,14},{3,15},{4,8},{5,9},{6,10},{7,11},{8,4},{9,5},... | collective-permute-start | bytes 1572872 | tf_op jit(solution)/shard_map/ppermute | solution.py:384
  179.9 0.8 copy-start.12
  189.3 0.8 copy-start.14
  190.1 2.2 copy-start.6
  192.3 1.0 copy-start.11
  193.4 1.0 copy-start.13
  194.4 1.0 copy-start.15
  195.5 17.3 %copy-start.7 = (bf16[2048,1024]{1,0:T(8,128)(2,1)S(1)}, bf16[2048,1024]{1,0:T(8,128)(2,1)}, u32[]{:S(2)}) copy-start(bf16[2048,1024]{1,0:T(8,128)(2,1)} %all-gather.3.cloned.1.call-done) | copy-start | bytes 12582916
  201.4 20.1 %collective-permute-start.11 = (bf16[512,2048]{1,0:T(8,128)(2,1)}, bf16[512,2048]{1,0:T(8,128)(2,1)}, u32[]{:S(2)}, u32[]{:S(2)}) collective-permute-start(bf16[512,2048]{1,0:T(8,128)(2,1)} %get-tuple-element.45), channel_id=1, source_target_pairs={{0,1},{1,0},{2,3},{3,2},{4,5},{5,4},{6,7},{7,6},{8,9},{9,8},{10,11... | collective-permute-start | bytes 6291464 | tf_op jit(solution)/shard_map/ppermute | solution.py:384
  220.1 1.3 copy-start.1
  221.4 4.5 %collective-permute-start.18 = (bf16[512,2048]{1,0:T(8,128)(2,1)}, bf16[512,2048]{1,0:T(8,128)(2,1)}, u32[]{:S(2)}, u32[]{:S(2)}) collective-permute-start(bf16[512,2048]{1,0:T(8,128)(2,1)} %get-tuple-element.47), channel_id=1, source_target_pairs={{0,1},{1,0},{2,3},{3,2},{4,5},{5,4},{6,7},{7,6},{8,9},{9,8},{10,11... | collective-permute-start | bytes 6291464 | tf_op jit(solution)/shard_map/ppermute | solution.py:384
  223.9 2.0 copy-start.2
  224.0 26.0 %collective-permute-start.12 = (bf16[512,1024]{1,0:T(8,128)(2,1)S(1)}, bf16[512,1024]{1,0:T(8,128)(2,1)S(1)}, u32[]{:S(2)}, u32[]{:S(2)}) collective-permute-start(bf16[512,1024]{1,0:T(8,128)(2,1)S(1)} %broadcast_select_fusion.1), channel_id=1, source_target_pairs={{0,2},{1,3},{2,0},{3,1},{4,6},{5,7},{6,4},{7,5},{8,10},{9,11},{10,... | collective-permute-start | bytes 3145736 | tf_op jit(solution)/shard_map/ppermute | solution.py:384
  228.4 43.6 %collective-permute-start.19 = (bf16[512,1024]{1,0:T(8,128)(2,1)S(1)}, bf16[512,1024]{1,0:T(8,128)(2,1)S(1)}, u32[]{:S(2)}, u32[]{:S(2)}) collective-permute-start(bf16[512,1024]{1,0:T(8,128)(2,1)S(1)} %broadcast_select_fusion), channel_id=1, source_target_pairs={{0,2},{1,3},{2,0},{3,1},{4,6},{5,7},{6,4},{7,5},{8,10},{9,11},{10,... | collective-permute-start | bytes 3145736 | tf_op jit(solution)/shard_map/ppermute | solution.py:384
  250.7 22.7 %collective-permute-start.13 = (bf16[256,1024]{1,0:T(8,128)(2,1)S(1)}, bf16[256,1024]{1,0:T(8,128)(2,1)S(1)}, u32[]{:S(2)}, u32[]{:S(2)}) collective-permute-start(bf16[256,1024]{1,0:T(8,128)(2,1)S(1)} %slice.53), channel_id=1, source_target_pairs={{1,8},{3,10},{5,12},{7,14},{8,1},{10,3},{12,5},{14,7},{17,24},{19,... | collective-permute-start | bytes 1572872 | tf_op jit(solution)/shard_map/ppermute | solution.py:384
  272.7 1.4 collective-permute-start.20
  273.5 9.2 %collective-permute-start.14 = (bf16[256,1024]{1,0:T(8,128)(2,1)S(1)}, bf16[256,1024]{1,0:T(8,128)(2,1)S(1)}, u32[]{:S(2)}, u32[]{:S(2)}) collective-permute-start(bf16[256,1024]{1,0:T(8,128)(2,1)S(1)} %get-tuple-element.51), channel_id=1, source_target_pairs={{0,4},{1,12},{2,6},{3,14},{4,0},{5,8},{6,2},{7,10},{8,5},{9,13},{1... | collective-permute-start | bytes 1572872 | tf_op jit(solution)/shard_map/ppermute | solution.py:384
  274.2 25.4 %collective-permute-start.21 = (bf16[256,1024]{1,0:T(8,128)(2,1)S(1)}, bf16[256,1024]{1,0:T(8,128)(2,1)S(1)}, u32[]{:S(2)}, u32[]{:S(2)}) collective-permute-start(bf16[256,1024]{1,0:T(8,128)(2,1)S(1)} %get-tuple-element.55), channel_id=1, source_target_pairs={{0,4},{1,12},{2,6},{3,14},{4,0},{5,8},{6,2},{7,10},{8,5},{9,13},{1... | collective-permute-start | bytes 1572872 | tf_op jit(solution)/shard_map/ppermute | solution.py:384
Sparse Core Ops, SparseCore 0:
  38.8 128.2 all-gather.2
